TPU v7x, 32 devices: a whole 2x2x4 slice. The times are simulated.
32 devices in a mesh: leaf: 2 (over x), blk: 4 (over y, core), kv: 4 (over z).
Axes of the slice: x: 2, y: 2, z: 4, core: 2. Of those that a mesh axis runs over, the one named last changes fastest.
Arguments:
- queries: bfloat16 [4096, 2560], P(('leaf', 'blk', 'kv')), parts along dimension 0, may hold values from -8 to 8
- keys: bfloat16 [16384, 512], P(('leaf', 'blk', 'kv')), parts along dimension 0, may hold values from -8 to 8
- values: bfloat16 [16384, 512], P(('leaf', 'blk', 'kv')), parts along dimension 0, may hold values from -6 to 6
- ancestry: int32 [32, 64], P('leaf'), parts along dimension 0, may hold values from 0 to 1, as said below
- leaf_tiles: int32 [32], P('leaf'), parts along dimension 0, may hold values from 1 to 63, as said below
Outputs:
- attended: bfloat16 [4096, 2560], P(('leaf', 'blk', 'kv')), parts along dimension 0
There are 2 independent parts, one for each index of `leaf`. A program takes and returns all parts, laid end to end along the dimension named above; each array names one. Nothing has to cross between parts.
Inputs may be any that keep to these rules, and one draw needn't show every extreme that they name: ancestry[a, t] is 1 exactly when key tile t is a strict ancestor of tile leaf_tiles[a] in the tree whose nodes are the key tiles; tile 0 is the root of the tree. `leaf_tiles`: strictly rising; the last entry is 63.
All inputs are finite; a program needn't handle non-finite values.
Results may differ from a plain program's by a relative error of at most 0.018.
Values may be sent and summed in bfloat16 or wider, within the bound.
A program may use at most 256 MiB of HBM per device.

v0:
```python
import math

import jax
import jax.numpy as jnp
from jax import lax
from jax.sharding import PartitionSpec as P

TILE = 128
KV_HEADS = 4
GROUP = 5
DH = 128


def row_tables(ancestry, leaf_tiles, first_row, row_count):
    query_ids = first_row + jnp.arange(row_count, dtype=jnp.int32)
    query_tiles = query_ids // TILE
    picker = (
        query_tiles[:, None] == jnp.arange(ancestry.shape[0], dtype=jnp.int32)[None, :]
    ).astype(jnp.float32)
    tile_rows = jnp.dot(picker, ancestry.astype(jnp.float32), precision=lax.Precision.HIGHEST)
    home_tile = jnp.dot(picker, leaf_tiles.astype(jnp.float32), precision=lax.Precision.HIGHEST)
    return (tile_rows, home_tile, query_ids % TILE)


def key_mask(tables, key_ids):
    tile_rows, home_tile, in_tile = tables
    key_tiles = key_ids // TILE
    picker = (
        key_tiles[:, None] == jnp.arange(tile_rows.shape[1], dtype=jnp.int32)[None, :]
    ).astype(jnp.float32)
    linked = jnp.dot(tile_rows, picker.T, precision=lax.Precision.HIGHEST) > 0.5
    own_tile = key_tiles.astype(jnp.float32)[None, :] == home_tile[:, None]
    causal = (key_ids % TILE)[None, :] <= in_tile[:, None]
    return jnp.where(own_tile, causal, linked)


def attend(carried, query_heads, key_piece, value_piece, allowed):
    row_peak, row_total, summed = carried
    scaling = 1.0 / math.sqrt(DH)
    key_heads = key_piece.reshape(key_piece.shape[0], KV_HEADS, DH)
    value_heads = value_piece.reshape(value_piece.shape[0], KV_HEADS, DH)
    scores = (
        jnp.einsum("qhgd,khd->hgqk", query_heads, key_heads, preferred_element_type=jnp.float32)
        * scaling
    )
    scores = jnp.where(allowed[None, None], scores, -1e30)
    new_peak = jnp.maximum(row_peak, jnp.max(scores, axis=-1))
    weights = jnp.where(allowed[None, None], jnp.exp(scores - new_peak[..., None]), 0.0)
    row_total = jnp.sum(weights, axis=-1)
    update = jnp.einsum(
        "hgqk,khd->qhgd",
        weights.astype(jnp.bfloat16),
        value_heads,
        preferred_element_type=jnp.float32,
    )
    summed = update
    return (new_peak, row_total, summed)


def block_step(tables, query_heads, key_ids_of, carried, pieces, offset):
    key_piece, value_piece = pieces
    allowed = key_mask(tables, key_ids_of(offset, key_piece.shape[0]))
    return attend(carried, query_heads, key_piece, value_piece, allowed)


def starting(row_count):
    return (
        jnp.full((KV_HEADS, GROUP, row_count), -1e30, jnp.float32),
        jnp.zeros((KV_HEADS, GROUP, row_count), jnp.float32),
        jnp.zeros((row_count, KV_HEADS, GROUP, DH), jnp.float32),
    )


def finish(row_total, summed):
    result = summed / jnp.transpose(row_total, (2, 0, 1))[..., None]
    return result.reshape(result.shape[0], KV_HEADS * GROUP * DH).astype(jnp.bfloat16)


def on_device(queries, keys, values, ancestry, leaf_tiles):
    own_rows = queries.shape[0]
    first_row = lax.axis_index(("blk", "kv")) * own_rows
    tables = row_tables(ancestry, leaf_tiles, first_row, own_rows)
    query_heads = queries.reshape(own_rows, KV_HEADS, GROUP, DH)

    def whole_ids(offset, length):
        return jnp.arange(length, dtype=jnp.int32)

    result = block_step(
        tables,
        query_heads,
        whole_ids,
        starting(own_rows),
        (
            lax.all_gather(keys, ("blk", "kv"), axis=0, tiled=True),
            lax.all_gather(values, ("blk", "kv"), axis=0, tiled=True),
        ),
        jnp.int32(0),
    )
    return finish(result[1], result[2])


def solution(mesh):
    in_specs = (
        P(("leaf", "blk", "kv"), None),
        P(("leaf", "blk", "kv"), None),
        P(("leaf", "blk", "kv"), None),
        P("leaf", None),
        P("leaf"),
    )
    out_specs = P(("leaf", "blk", "kv"), None)
    return jax.shard_map(
        on_device, mesh=mesh, in_specs=in_specs, out_specs=out_specs, check_vma=False
    )
```

profile of v0, /device:TPU:0, one launch (start us, length us, event | category | flops | bytes accessed | tf_op | source)
XLA Modules:
  0.0 218.7 jit_solution(985103688343570723)
XLA Ops:
  6.5 0.0 all-gather.3.cloned.1.call-start
  6.5 2.0 copy.20
  8.6 0.0 all-gather.3.cloned.1.call-update
  8.6 0.0 all-gather.5.cloned.1.call-start
  8.7 0.7 all-gather.5.cloned.1.call-update
  9.4 0.8 convolution_bitcast_fusion
  10.2 0.1 fusion.14
  10.3 1.0 fusion.13
  11.3 2.8 %fusion.6 = pred[128,8192]{1,0:T(8,128)(4,1)S(1)} fusion(f32[128,64]{0,1:T(8,128)S(1)} %fusion.13, s32[8192]{0:T(1024)S(1)} %get-tuple-element.9, f32[8192]{0:T(1024)S(1)} %fusion.23, s32[128]{0:T(128)S(1)} %get-tuple-element.7, f32[128]{0:T(128)S(1)} %convolution_bitcast_fusion, s32[8192]{0:T(1024)S(1)} %get-tuple-element.10), kind=kOutput, calls=%fused_computation.8 | convolution fusion | flops 810024960 | bytes 1180672 | tf_op jit(solution)/shard_map/dot_general | solution.py:31
  14.1 2.5 %copy.19 = pred[128,8192]{0,1:T(8,128)(4,1)S(1)} copy(pred[128,8192]{1,0:T(8,128)(4,1)S(1)} %fusion.6) | data formatting | bytes 2097152 | tf_op jit(solution)/shard_map/jit(_where)/select_n | solution.py:34
  16.6 1.4 copy.21
  18.0 72.3 %all-gather.3.cloned.1.call-done = bf16[8192,512]{0,1:T(8,128)(2,1)} async-done(((bf16[512,512]{0,1:T(8,128)(2,1)}), bf16[8192,512]{0,1:T(8,128)(2,1)}) %all-gather.3.cloned.1.call-update) | async-done | bytes 8388624 | tf_op jit(solution)/shard_map/all_gather | solution.py:94
  90.3 32.9 %fusion = (f32[4,5,128]{2,1,0:T(8,128)S(1)}, f32[4,8192,128,5]{2,1,3,0:T(8,128)}) fusion(pred[128,8192]{0,1:T(8,128)(4,1)S(1)} %copy.19, bf16[8192,4,128,1]{0,2,3,1:T(8,128)(2,1)} %bitcast.45, bf16[128,4,5,128]{0,3,2,1:T(8,128)(2,1)S(1)} %bitcast.42), kind=kOutput, calls=%fused_computation.2 | convolution fusion | flops 5431621120 | bytes 93988864 | tf_op jit(solution)/shard_map/qhgd,khd->hgqk/dot_general | solution.py:43
  123.2 27.6 %fusion.1 = f32[4,5,128]{2,1,0:T(8,128)S(1)} fusion(f32[4,8192,128,5]{2,1,3,0:T(8,128)} %get-tuple-element.6, f32[4,5,128]{2,1,0:T(8,128)S(1)} %broadcast_maximum_fusion, pred[128,8192]{0,1:T(8,128)(4,1)S(1)} %copy.19), kind=kLoop, calls=%fused_computation.3 | loop fusion | flops 104855040 | bytes 84955136 | tf_op jit(solution)/shard_map/reduce_sum | solution.py:49
  150.8 14.7 %all-gather.5.cloned.1.call-done = bf16[8192,512]{1,0:T(8,128)(2,1)} async-done(((bf16[512,512]{1,0:T(8,128)(2,1)}), bf16[8192,512]{1,0:T(8,128)(2,1)}) %all-gather.5.cloned.1.call-update) | async-done | bytes 8388624 | tf_op jit(solution)/shard_map/all_gather | solution.py:95
  165.6 12.0 %copy.24 = bf16[8192,512]{0,1:T(8,128)(2,1)} copy(bf16[8192,512]{1,0:T(8,128)(2,1)} %all-gather.5.cloned.1.call-done) | data formatting | bytes 16777216 | tf_op jit(solution)/shard_map/all_gather | solution.py:95
  177.6 33.2 %divide_convert_fusion = bf16[128,4,5,128]{0,3,2,1:T(8,128)(2,1)S(1)} fusion(bf16[8192,4,128,1]{0,2,3,1:T(8,128)(2,1)} %bitcast.41, f32[4,8192,128,5]{2,1,3,0:T(8,128)} %get-tuple-element.6, f32[4,5,128]{2,1,0:T(8,128)S(1)} %broadcast_maximum_fusion, pred[128,8192]{0,1:T(8,128)(4,1)S(1)} %copy.19, f32[128,4,5]{0,2,1:T(8,128)S(1)} %bitcast.44), kind=kOutput, calls=%fused_computation.11 | convolution fusion | flops 5474222080 | bytes 93999104 | tf_op jit(solution)/shard_map/hgqk,khd->qhgd/dot_general | solution.py:50
  210.7 1.1 copy.26
  (3 shorter events, 0.0 us)
Async XLA Ops:
  6.5 83.7 %all-gather.3.cloned.1.call-start = ((), (), s32[]{:S(2)}) async-start(), calls=%async_computation | async-start | bytes 8912896 | tf_op jit(solution)/shard_map/all_gather | solution.py:94
  8.6 157.0 %all-gather.5.cloned.1.call-start = ((), (), s32[]{:S(2)}) async-start(), calls=%async_computation.1 | async-start | bytes 8912896 | tf_op jit(solution)/shard_map/all_gather | solution.py:95
Sparse Core Ops, SparseCore 0:
  9.4 80.7 all-gather.2
  92.5 73.0 all-gather.4
where the time goes:
time: 219 us
  waiting for transfers between devices  87.7 us (40%)
  matrix products  70.7 us (32%)
  other arithmetic  27.7 us (13%)
  local copies, waits for them, and re-layouts  19.1 us (9%)
  between operations  13.5 us (6%)
    all_gather x1, waiting for transfers between devices, on_device(): lax.all_gather(keys, ('blk', 'kv'), axis=0, tiled=True)  72.3 us
    dot_general x1, matrix products, attend(): jnp.einsum('hgqk,khd->qhgd', weights.astype(jnp.bfloat16), value_heads, p...  33.2 us
    dot_general x1, matrix products, attend(): jnp.einsum('qhgd,khd->hgqk', query_heads, key_heads, preferred_element_ty...  32.9 us
    reduce_sum x1, other arithmetic, attend(): row_total = jnp.sum(weights, axis=-1)  27.6 us
    all_gather x1, waiting for transfers between devices, on_device(): lax.all_gather(values, ('blk', 'kv'), axis=0, tiled=True)  14.7 us
    all_gather x1, local copies, waits for them, and re-layouts, on_device(): lax.all_gather(values, ('blk', 'kv'), axis=0, tiled=True)  12 us
  transfers between devices with their start and end apart: 2, of which 2 were waited for; matrix products, arithmetic and copies ran while one was open for 32% of the time, Pallas kernels for 0%

commit v1 on v0

v1 whole, which is shorter than its diff:
```python
import functools
import math

import jax
import jax.numpy as jnp
from jax import lax
from jax.experimental import pallas as pl
from jax.experimental.pallas import tpu as pltpu
from jax.sharding import PartitionSpec as P

TILE = 128
KV_HEADS = 4
GROUP = 5
DH = 128
WIDE = GROUP * DH
MESH = pl.DeviceIdType.MESH
NEG = -1e30
EXP2_SCALE = math.log2(math.e) / math.sqrt(DH)

KV_OFFSETS = ((0, 3), (1, 3), (0, 2), (1, 2), (1, 1), (0, 1), (1, 0))
GROUP_OFFSETS = ((1, 1), (0, 1), (1, 0))


class Place:
    def __init__(self):
        self.leaf = lax.axis_index("leaf")
        self.blk = lax.axis_index("blk")
        self.z = lax.axis_index("kv")
        self.y = self.blk // 2
        self.core = self.blk % 2

    def partner(self, dy, dz):
        y = 1 - self.y if dy else self.y
        z = self.z
        if dz == 1:
            z = z + 1 - 2 * (z % 2)
        elif dz == 2:
            z = (z + 2) % 4
        elif dz == 3:
            z = 3 - z
        return y, z

    def device(self, y, core, z):
        return (self.leaf, 2 * y + core, z)


def head_of(y, z):
    return 2 * y + z % 2


def aligned(index, size):
    return pl.ds(pl.multiple_of(index * size, size), size)


def greet(devices):
    barrier = pltpu.get_barrier_semaphore()
    for device in devices:
        pl.semaphore_signal(barrier, inc=1, device_id=device, device_id_type=MESH)
    pl.semaphore_wait(barrier, len(devices))


def gather_kernel(
    q_ref, k_ref, v_ref, q_all, k_all, v_all,
    kv_send, kv_recv, pass_send, pass_recv, q_send, q_recv, own_sem,
):
    at = Place()
    rows = k_ref.shape[0]
    sibling = at.device(at.y, 1 - at.core, at.z)
    partners = [at.partner(dy, dz) for dy, dz in KV_OFFSETS]
    greet([at.device(y, at.core, z) for y, z in partners] + [sibling])

    head = head_of(at.y, at.z)
    here = aligned(at.blk * 4 + at.z, rows)

    def rows_of(y, core, z):
        return aligned((2 * y + core) * 4 + z, rows)

    kv = ((k_ref, k_all), (v_ref, v_all))

    def send_kv(i):
        y, z = partners[i]
        copies = []
        for w, (own, whole) in enumerate(kv):
            copies.append(
                pltpu.make_async_remote_copy(
                    src_ref=own.at[:, aligned(head_of(y, z), DH)],
                    dst_ref=whole.at[here],
                    send_sem=kv_send.at[2 * i + w],
                    recv_sem=kv_recv.at[2 * i + w],
                    device_id=at.device(y, at.core, z),
                    device_id_type=MESH,
                )
            )
        return copies

    def arrive_kv(i):
        y, z = partners[i]
        return [
            pltpu.make_async_remote_copy(
                src_ref=own.at[:, aligned(head, DH)],
                dst_ref=whole.at[rows_of(y, at.core, z)],
                send_sem=kv_send.at[2 * i + w],
                recv_sem=kv_recv.at[2 * i + w],
                device_id=at.device(y, at.core, z),
                device_id_type=MESH,
            )
            for w, (own, whole) in enumerate(kv)
        ]

    def send_q(i):
        y, z = at.partner(*GROUP_OFFSETS[i])
        return pltpu.make_async_remote_copy(
            src_ref=q_ref.at[:, aligned(head_of(y, z), WIDE)],
            dst_ref=q_all.at[aligned(head, TILE)],
            send_sem=q_send.at[i],
            recv_sem=q_recv.at[i],
            device_id=at.device(y, at.core, z),
            device_id_type=MESH,
        )

    def arrive_q(i):
        y, z = at.partner(*GROUP_OFFSETS[i])
        return pltpu.make_async_remote_copy(
            src_ref=q_ref.at[:, aligned(head, WIDE)],
            dst_ref=q_all.at[aligned(head_of(y, z), TILE)],
            send_sem=q_send.at[i],
            recv_sem=q_recv.at[i],
            device_id=at.device(y, at.core, z),
            device_id_type=MESH,
        )

    def pass_on(i, source, rows_here):
        return [
            pltpu.make_async_remote_copy(
                src_ref=source[w],
                dst_ref=kv[w][1].at[rows_here],
                send_sem=pass_send.at[2 * i + w],
                recv_sem=pass_recv.at[2 * i + w],
                device_id=sibling,
                device_id_type=MESH,
            )
            for w in range(2)
        ]

    sends = []
    for i in range(len(KV_OFFSETS)):
        if i == 4:
            for j in range(3):
                sends.append(send_q(j))
                sends[-1].start()
        for copy in send_kv(i):
            copy.start()
            sends.append(copy)

    mine = [own.at[:, aligned(head, DH)] for own, _ in kv]
    last = len(KV_OFFSETS)
    for copy in pass_on(last, mine, here):
        copy.start()
        sends.append(copy)
    locals_ = [
        pltpu.make_async_copy(mine[w], kv[w][1].at[here], own_sem.at[w]) for w in range(2)
    ] + [
        pltpu.make_async_copy(
            q_ref.at[:, aligned(head, WIDE)], q_all.at[aligned(head, TILE)], own_sem.at[2]
        )
    ]
    for copy in locals_:
        copy.start()

    for i in (6, 5, 4, 0, 1, 2, 3):
        y, z = partners[i]
        came = rows_of(y, at.core, z)
        onward = pass_on(i, [whole.at[came] for _, whole in kv], came)
        for arrival, copy in zip(arrive_kv(i), onward):
            arrival.wait_recv()
            copy.start()
            sends.append(copy)

    for copy in locals_:
        copy.wait()
    for j in range(3):
        arrive_q(j).wait_recv()
    for i in range(last + 1):
        y, z = partners[i] if i < last else (at.y, at.z)
        came = rows_of(y, 1 - at.core, z)
        for copy in pass_on(i, [whole.at[came] for _, whole in kv], came):
            copy.wait_recv()
    for copy in sends:
        copy.wait_send()


def attend_kernel(
    ancestry, leaf_tiles, q_ref, k_hbm, v_hbm, out_ref,
    k_ref, v_ref, scores, peak_ref, total_ref, sum_ref, visits, sems,
):
    at = Place()
    half = at.z // 2
    k_copy = pltpu.make_async_copy(k_hbm, k_ref, sems.at[0])
    v_copy = pltpu.make_async_copy(v_hbm, v_ref, sems.at[1])
    k_copy.start()
    v_copy.start()

    tile_ids = [(2 * (j // 2) + at.core) * 4 + half * 2 + j % 2 for j in range(4)]
    homes = [leaf_tiles[a] for a in tile_ids]
    for j in range(4):
        visits[j, 0] = homes[j]

    def look(t, counts):
        after = []
        for j in range(4):
            visits[j, counts[j]] = t
            hit = jnp.logical_and(ancestry[tile_ids[j], t] == 1, t != homes[j])
            after.append(counts[j] + jnp.where(hit, 1, 0))
        return tuple(after)

    counts = lax.fori_loop(0, ancestry.shape[1], look, (jnp.int32(1),) * 4)
    for j in range(4):
        visits[j, counts[j]] = 0

    k_copy.wait()
    v_copy.wait()

    def pair_of(ref, j, i):
        first = ref[aligned(visits[j, 2 * i], TILE), :]
        second = ref[aligned(visits[j, 2 * i + 1], TILE), :]
        return jnp.concatenate([first, second], axis=0)

    for j in range(4):
        rows = pl.ds(j * TILE, TILE)
        query = jnp.concatenate(
            [q_ref[rows, pl.ds(g * DH, DH)] for g in range(GROUP)], axis=0
        )
        count = counts[j]
        steps = (count + 1) // 2

        def score(i, first):
            raw = lax.dot_general(
                query, pair_of(k_ref, j, i), (((1,), (1,)), ((), ())),
                preferred_element_type=jnp.float32,
            )
            left = raw[:, :TILE]
            if first:
                q_in = lax.broadcasted_iota(jnp.int32, (WIDE, TILE), 0) % TILE
                s_in = lax.broadcasted_iota(jnp.int32, (WIDE, TILE), 1)
                left = jnp.where(s_in <= q_in, left, NEG)
            right = raw[:, TILE:] + jnp.where(2 * i + 1 < count, 0.0, NEG)
            scores[i, :, :TILE] = left
            scores[i, :, TILE:] = right
            best = jnp.maximum(left, right)
            peak_ref[...] = best if first else jnp.maximum(peak_ref[...], best)

        score(0, True)

        @pl.loop(1, steps)
        def _(i):
            score(i, False)

        peak_ref[...] = jnp.broadcast_to(
            jnp.max(peak_ref[...], axis=1, keepdims=True), peak_ref.shape
        )

        def weigh(i, first):
            peak = peak_ref[...]
            left = jnp.exp2((scores[i, :, :TILE] - peak) * EXP2_SCALE)
            right = jnp.exp2((scores[i, :, TILE:] - peak) * EXP2_SCALE)
            rounded = jnp.concatenate(
                [left.astype(jnp.bfloat16), right.astype(jnp.bfloat16)], axis=1
            )
            update = jnp.dot(rounded, pair_of(v_ref, j, i), preferred_element_type=jnp.float32)
            both = left + right
            total_ref[...] = both if first else total_ref[...] + both
            sum_ref[...] = update if first else sum_ref[...] + update

        weigh(0, True)

        @pl.loop(1, steps)
        def _(i):
            weigh(i, False)

        result = sum_ref[...] / jnp.sum(total_ref[...], axis=1, keepdims=True)
        for g in range(GROUP):
            out_ref[rows, pl.ds(g * DH, DH)] = result[g * TILE : (g + 1) * TILE].astype(
                jnp.bfloat16
            )


def return_kernel(part_ref, out_ref, send_sem, recv_sem, own_sem):
    at = Place()
    head = head_of(at.y, at.z)
    partners = [at.partner(dy, dz) for dy, dz in GROUP_OFFSETS]
    greet([at.device(y, at.core, z) for y, z in partners])
    own = pltpu.make_async_copy(
        part_ref.at[aligned(head, TILE)], out_ref.at[:, aligned(head, WIDE)], own_sem
    )
    sends, arrivals = [], []
    for i, (y, z) in enumerate(partners):
        there = head_of(y, z)
        common = dict(
            src_ref=part_ref.at[aligned(there, TILE)],
            send_sem=send_sem.at[i],
            recv_sem=recv_sem.at[i],
            device_id=at.device(y, at.core, z),
            device_id_type=MESH,
        )
        sends.append(
            pltpu.make_async_remote_copy(dst_ref=out_ref.at[:, aligned(head, WIDE)], **common)
        )
        arrivals.append(
            pltpu.make_async_remote_copy(dst_ref=out_ref.at[:, aligned(there, WIDE)], **common)
        )
    for copy in sends:
        copy.start()
    own.start()
    own.wait()
    for copy in arrivals:
        copy.wait_recv()
    for copy in sends:
        copy.wait_send()


def on_device(group_size, queries, keys, values, ancestry, leaf_tiles):
    rows = queries.shape[0]
    total_keys = keys.shape[0] * group_size
    any_space = pl.BlockSpec(memory_space=pl.ANY)
    vmem = pl.BlockSpec(memory_space=pltpu.VMEM)
    smem = pl.BlockSpec(memory_space=pltpu.SMEM)
    dma = pltpu.SemaphoreType.DMA
    bf16 = jnp.bfloat16
    n = len(KV_OFFSETS)
    q_all, k_all, v_all = pl.pallas_call(
        gather_kernel,
        out_shape=(
            jax.ShapeDtypeStruct((4 * rows, WIDE), bf16),
            jax.ShapeDtypeStruct((total_keys, DH), bf16),
            jax.ShapeDtypeStruct((total_keys, DH), bf16),
        ),
        in_specs=[any_space] * 3,
        out_specs=[any_space] * 3,
        scratch_shapes=[
            dma((2 * n,)), dma((2 * n,)), dma((2 * n + 2,)), dma((2 * n + 2,)),
            dma((3,)), dma((3,)), dma((3,)),
        ],
        compiler_params=pltpu.CompilerParams(collective_id=0, has_side_effects=True),
        name="gather_heads",
    )(queries, keys, values)

    tiles = total_keys // TILE
    part = pl.pallas_call(
        attend_kernel,
        out_shape=jax.ShapeDtypeStruct((4 * rows, WIDE), bf16),
        in_specs=[smem, smem, vmem, any_space, any_space],
        out_specs=vmem,
        scratch_shapes=[
            pltpu.VMEM((total_keys, DH), bf16),
            pltpu.VMEM((total_keys, DH), bf16),
            pltpu.VMEM((tiles // 2, WIDE, 2 * TILE), jnp.float32),
            pltpu.VMEM((WIDE, TILE), jnp.float32),
            pltpu.VMEM((WIDE, TILE), jnp.float32),
            pltpu.VMEM((WIDE, DH), jnp.float32),
            pltpu.SMEM((4, 128), jnp.int32),
            dma((2,)),
        ],
        compiler_params=pltpu.CompilerParams(vmem_limit_bytes=48 * 1024 * 1024),
        name="attend_tree",
    )(ancestry, leaf_tiles, q_all, k_all, v_all)

    return pl.pallas_call(
        return_kernel,
        out_shape=jax.ShapeDtypeStruct((rows, KV_HEADS * WIDE), bf16),
        in_specs=[any_space],
        out_specs=any_space,
        scratch_shapes=[dma((3,)), dma((3,)), dma],
        compiler_params=pltpu.CompilerParams(collective_id=1, has_side_effects=True),
        name="return_heads",
    )(part)


def solution(mesh):
    in_specs = (
        P(("leaf", "blk", "kv"), None),
        P(("leaf", "blk", "kv"), None),
        P(("leaf", "blk", "kv"), None),
        P("leaf", None),
        P("leaf"),
    )
    out_specs = P(("leaf", "blk", "kv"), None)
    group_size = mesh.shape["blk"] * mesh.shape["kv"]
    return jax.shard_map(
        functools.partial(on_device, group_size),
        mesh=mesh, in_specs=in_specs, out_specs=out_specs, check_vma=False,
    )
```

time: 219 us -> 85 us (0.39)
  waiting for transfers between devices: 87.7 us -> 0 us
  Pallas kernels: 0 us -> 76.3 us
  matrix products: 70.7 us -> 0 us
  other arithmetic: 27.7 us -> 0 us
  between operations: 13.5 us -> 0.05 us
  local copies, waits for them, and re-layouts: 19.1 us -> 8.41 us
    all_gather x2 -> x0, waiting for transfers between devices: 87 us -> none  [the longest x1 72.3 us: on_device(): lax.all_gather(keys, ('blk', 'kv'), axis=0, tiled=True)]
    pallas_call x0 -> x3, Pallas kernels: none -> 76.3 us  [the longest x1 56.5 us: on_device(): pl.pallas_call(gather_kernel, out_shape=(jax.ShapeDtypeStruct((4 * rows,...]
    dot_general x5 -> x0, matrix products: 70.7 us -> none  [the longest x1 33.2 us: attend(): jnp.einsum('hgqk,khd->qhgd', weights.astype(jnp.bfloat16), value_heads, p...]
    reduce_sum x1 -> x0, other arithmetic: 27.6 us -> none  [attend(): row_total = jnp.sum(weights, axis=-1)]
    all_gather x1 -> x0, local copies, waits for them, and re-layouts: 12 us -> none  [on_device(): lax.all_gather(values, ('blk', 'kv'), axis=0, tiled=True)]
    unnamed x2 -> x13, local copies, waits for them, and re-layouts: 3.46 us -> 8.41 us
    select_n x1 -> x0, local copies, waits for them, and re-layouts: 2.49 us -> none  [key_mask(): return jnp.where(own_tile, causal, linked)]
  transfers between devices with their start and end apart: 2 -> 0, of which waited for: 2 -> 0; matrix products, arithmetic and copies ran while one was open for 32% -> 0% of each run, Pallas kernels for 0% -> 0%
where the time goes in v1:
time: 85 us; the launch traced here: 84.8 us
  Pallas kernels  76.3 us (90%)
  local copies, waits for them, and re-layouts  8.41 us (10%)
    pallas_call x1, Pallas kernels, on_device(): pl.pallas_call(gather_kernel, out_shape=(jax.ShapeDtypeStruct((4 * rows,...  56.5 us
    pallas_call x1, Pallas kernels, on_device(): pl.pallas_call(return_kernel, out_shape=jax.ShapeDtypeStruct((rows, KV_HE...  11.3 us
    pallas_call x1, Pallas kernels, on_device(): pl.pallas_call(attend_kernel, out_shape=jax.ShapeDtypeStruct((4 * rows, W...  8.57 us
    unnamed x13, local copies, waits for them, and re-layouts  8.41 us

profile of v1, /device:TPU:0, one launch (start us, length us, event | category | flops | bytes accessed | tf_op | source)
XLA Modules:
  0.0 84.8 jit_solution(8701675378863266503)
XLA Ops:
  0.0 56.5 %gather_heads.1 = (bf16[512,640]{1,0:T(8,128)(2,1)}, bf16[8192,128]{1,0:T(8,128)(2,1)}, bf16[8192,128]{1,0:T(8,128)(2,1)}) custom-call(bf16[128,2560]{1,0:T(8,128)(2,1)} %q_ref.1, bf16[512,512]{1,0:T(8,128)(2,1)} %k_ref.1, bf16[512,512]{1,0:T(8,128)(2,1)} %v_ref.1), custom_call_target="tpu_custom_call" | custom-call | tf_op jit(solution)/shard_map/gather_heads/pallas_call | solution.py:330
  56.5 0.0 copy-start.1
  56.5 1.6 %copy-done.1 = bf16[8192,128]{1,0:T(8,128)(2,1)S(1)} copy-done((bf16[8192,128]{1,0:T(8,128)(2,1)S(1)}, bf16[8192,128]{1,0:T(8,128)(2,1)}, u32[]{:S(2)}) %copy-start.1) | copy-done | bytes 2097176
  58.1 0.0 copy-start.2
  58.1 1.6 %copy-done.2 = bf16[8192,128]{1,0:T(8,128)(2,1)S(1)} copy-done((bf16[8192,128]{1,0:T(8,128)(2,1)S(1)}, bf16[8192,128]{1,0:T(8,128)(2,1)}, u32[]{:S(2)}) %copy-start.2) | copy-done | bytes 2097176
  59.7 0.0 copy-start.3
  59.7 1.1 %copy-done.3 = bf16[512,640]{1,0:T(8,128)(2,1)S(1)} copy-done((bf16[512,640]{1,0:T(8,128)(2,1)S(1)}, bf16[512,640]{1,0:T(8,128)(2,1)}, u32[]{:S(2)}) %copy-start.3) | copy-done | bytes 655384
  60.8 0.0 copy-start.4
  60.8 0.7 copy-done.4
  61.5 0.0 copy-start.5
  61.5 0.7 copy-done.5
  62.1 8.6 %attend_tree.1.part_ref = bf16[512,640]{1,0:T(8,128)(2,1)S(1)} custom-call(s32[16,64]{1,0:T(8,128)S(1)} %copy-done.4, s32[16]{0:T(128)S(1)} %copy-done.5, bf16[512,640]{1,0:T(8,128)(2,1)S(1)} %copy-done.3, bf16[8192,128]{1,0:T(8,128)(2,1)S(1)} %copy-done.1, bf16[8192,128]{1,0:T(8,128)(2,1)S(1)} %copy-done.2), custom_call_target="tpu_custom_call" | custom-call | tf_op jit(solution)/shard_map/attend_tree/pallas_call | solution.py:348
  70.7 0.0 copy-start
  70.7 0.8 copy-done
  71.5 11.3 %return_heads.1 = bf16[128,2560]{1,0:T(8,128)(2,1)} custom-call(bf16[512,640]{1,0:T(8,128)(2,1)} %copy-done), custom_call_target="tpu_custom_call" | custom-call | tf_op jit(solution)/shard_map/return_heads/pallas_call | solution.py:367
  82.8 2.0 %copy.7 = bf16[128,2560]{1,0:T(8,128)(2,1)} copy(bf16[128,2560]{1,0:T(8,128)(2,1)} %return_heads.1) | data formatting | bytes 1310720
Async XLA Ops:
  56.5 1.6 %copy-start.1 = (bf16[8192,128]{1,0:T(8,128)(2,1)S(1)}, bf16[8192,128]{1,0:T(8,128)(2,1)}, u32[]{:S(2)}) copy-start(bf16[8192,128]{1,0:T(8,128)(2,1)} %get-tuple-element.9.k_hbm) | copy-start | bytes 6291460
  58.1 1.6 %copy-start.2 = (bf16[8192,128]{1,0:T(8,128)(2,1)S(1)}, bf16[8192,128]{1,0:T(8,128)(2,1)}, u32[]{:S(2)}) copy-start(bf16[8192,128]{1,0:T(8,128)(2,1)} %get-tuple-element.10.v_hbm) | copy-start | bytes 6291460
  59.7 1.1 %copy-start.3 = (bf16[512,640]{1,0:T(8,128)(2,1)S(1)}, bf16[512,640]{1,0:T(8,128)(2,1)}, u32[]{:S(2)}) copy-start(bf16[512,640]{1,0:T(8,128)(2,1)} %get-tuple-element.8.q_ref) | copy-start | bytes 1966084
  60.8 0.7 copy-start.4
  61.5 0.7 copy-start.5
  70.7 0.8 copy-start

commit v2 on v1

--- a/solution.py
+++ b/solution.py
@@ -190,13 +190,15 @@
 
 
 def attend_kernel(
-    ancestry, leaf_tiles, q_ref, k_hbm, v_hbm, out_ref,
-    k_ref, v_ref, scores, peak_ref, total_ref, sum_ref, visits, sems,
+    ancestry, leaf_tiles, q_hbm, k_hbm, v_hbm, out_ref,
+    q_ref, k_ref, v_ref, scores, peak_ref, total_ref, sum_ref, visits, sems,
 ):
     at = Place()
     half = at.z // 2
     k_copy = pltpu.make_async_copy(k_hbm, k_ref, sems.at[0])
     v_copy = pltpu.make_async_copy(v_hbm, v_ref, sems.at[1])
+    q_copy = pltpu.make_async_copy(q_hbm, q_ref, sems.at[2])
+    q_copy.start()
     k_copy.start()
     v_copy.start()
 
@@ -213,10 +215,11 @@
             after.append(counts[j] + jnp.where(hit, 1, 0))
         return tuple(after)
 
-    counts = lax.fori_loop(0, ancestry.shape[1], look, (jnp.int32(1),) * 4)
+    counts = lax.fori_loop(0, ancestry.shape[1], look, (jnp.int32(1),) * 4, unroll=4)
     for j in range(4):
         visits[j, counts[j]] = 0
 
+    q_copy.wait()
     k_copy.wait()
     v_copy.wait()
 
@@ -340,7 +343,9 @@
             dma((2 * n,)), dma((2 * n,)), dma((2 * n + 2,)), dma((2 * n + 2,)),
             dma((3,)), dma((3,)), dma((3,)),
         ],
-        compiler_params=pltpu.CompilerParams(collective_id=0, has_side_effects=True),
+        compiler_params=pltpu.CompilerParams(
+            collective_id=0, has_side_effects=True, vmem_limit_bytes=60 * 1024 * 1024
+        ),
         name="gather_heads",
     )(queries, keys, values)
 
@@ -348,9 +353,10 @@
     part = pl.pallas_call(
         attend_kernel,
         out_shape=jax.ShapeDtypeStruct((4 * rows, WIDE), bf16),
-        in_specs=[smem, smem, vmem, any_space, any_space],
+        in_specs=[smem, smem, any_space, any_space, any_space],
         out_specs=vmem,
         scratch_shapes=[
+            pltpu.VMEM((4 * rows, WIDE), bf16),
             pltpu.VMEM((total_keys, DH), bf16),
             pltpu.VMEM((total_keys, DH), bf16),
             pltpu.VMEM((tiles // 2, WIDE, 2 * TILE), jnp.float32),
@@ -358,9 +364,9 @@
             pltpu.VMEM((WIDE, TILE), jnp.float32),
             pltpu.VMEM((WIDE, DH), jnp.float32),
             pltpu.SMEM((4, 128), jnp.int32),
-            dma((2,)),
+            dma((3,)),
         ],
-        compiler_params=pltpu.CompilerParams(vmem_limit_bytes=48 * 1024 * 1024),
+        compiler_params=pltpu.CompilerParams(vmem_limit_bytes=60 * 1024 * 1024),
         name="attend_tree",
     )(ancestry, leaf_tiles, q_all, k_all, v_all)
 
@@ -370,7 +376,9 @@
         in_specs=[any_space],
         out_specs=any_space,
         scratch_shapes=[dma((3,)), dma((3,)), dma],
-        compiler_params=pltpu.CompilerParams(collective_id=1, has_side_effects=True),
+        compiler_params=pltpu.CompilerParams(
+            collective_id=1, has_side_effects=True, vmem_limit_bytes=60 * 1024 * 1024
+        ),
         name="return_heads",
     )(part)
 

time: 85 us -> 82.3 us (0.968)
  local copies, waits for them, and re-layouts: 8.41 us -> 1.97 us
  Pallas kernels: 76.3 us -> 80 us
    unnamed x13 -> x1, local copies, waits for them, and re-layouts: 8.41 us -> 1.97 us
    pallas_call x1, Pallas kernels: 8.57 us -> 11.2 us  [on_device(): pl.pallas_call(attend_kernel, out_shape=jax.ShapeDtypeStruct((4 * rows, W...]
    pallas_call x1, Pallas kernels: 11.3 us -> 12.3 us  [on_device(): pl.pallas_call(return_kernel, out_shape=jax.ShapeDtypeStruct((rows, KV_HE...]
where the time goes in v2:
time: 82.3 us; the launch traced here: 82 us
  Pallas kernels  80 us (97%)
  local copies, waits for them, and re-layouts  1.97 us (2%)
    pallas_call x1, Pallas kernels, on_device(): pl.pallas_call(gather_kernel, out_shape=(jax.ShapeDtypeStruct((4 * rows,...  56.5 us
    pallas_call x1, Pallas kernels, on_device(): pl.pallas_call(return_kernel, out_shape=jax.ShapeDtypeStruct((rows, KV_HE...  12.3 us
    pallas_call x1, Pallas kernels, on_device(): pl.pallas_call(attend_kernel, out_shape=jax.ShapeDtypeStruct((4 * rows, W...  11.2 us
    unnamed x1, local copies, waits for them, and re-layouts  1.97 us

profile of v2, /device:TPU:0, one launch (start us, length us, event | category | flops | bytes accessed | tf_op | source)
XLA Modules:
  0.0 82.0 jit_solution(1402823398756086128)
XLA Ops:
  0.0 56.5 %gather_heads.1 = (bf16[512,640]{1,0:T(8,128)(2,1)}, bf16[8192,128]{1,0:T(8,128)(2,1)}, bf16[8192,128]{1,0:T(8,128)(2,1)}) custom-call(bf16[128,2560]{1,0:T(8,128)(2,1)} %q_ref.1, bf16[512,512]{1,0:T(8,128)(2,1)} %k_ref.1, bf16[512,512]{1,0:T(8,128)(2,1)} %v_ref.1), custom_call_target="tpu_custom_call" | custom-call | tf_op jit(solution)/shard_map/gather_heads/pallas_call | solution.py:333
  56.5 11.2 %attend_tree.1.part_ref = bf16[512,640]{1,0:T(8,128)(2,1)} custom-call(s32[16,64]{1,0:T(8,128)} %ancestry.1, s32[16]{0:T(128)} %leaf_tiles.1, bf16[512,640]{1,0:T(8,128)(2,1)} %get-tuple-element.8.q_hbm, bf16[8192,128]{1,0:T(8,128)(2,1)} %get-tuple-element.9.k_hbm, bf16[8192,128]{1,0:T(8,128)(2,1)} %get-tuple-element.10.v_hbm), custom_call_target="tpu_custom_call" | custom-call | tf_op jit(solution)/shard_map/attend_tree/pallas_call | solution.py:353
  67.7 12.3 %return_heads.1 = bf16[128,2560]{1,0:T(8,128)(2,1)} custom-call(bf16[512,640]{1,0:T(8,128)(2,1)} %attend_tree.1.part_ref), custom_call_target="tpu_custom_call" | custom-call | tf_op jit(solution)/shard_map/return_heads/pallas_call | solution.py:373
  80.0 2.0 %copy.7 = bf16[128,2560]{1,0:T(8,128)(2,1)} copy(bf16[128,2560]{1,0:T(8,128)(2,1)} %return_heads.1) | data formatting | bytes 1310720

commit v3 on v1

--- a/solution.py
+++ b/solution.py
@@ -189,44 +189,38 @@
         copy.wait_send()
 
 
-def attend_kernel(
-    ancestry, leaf_tiles, q_ref, k_hbm, v_hbm, out_ref,
-    k_ref, v_ref, scores, peak_ref, total_ref, sum_ref, visits, sems,
-):
+def attend_kernel(offsets, ancestry, leaf_tiles, q_ref, k_ref, v_ref, *refs):
+    outs = refs[: len(offsets)]
+    scores, peak_ref, total_ref, sum_ref, visits = refs[len(offsets) :]
     at = Place()
-    half = at.z // 2
-    k_copy = pltpu.make_async_copy(k_hbm, k_ref, sems.at[0])
-    v_copy = pltpu.make_async_copy(v_hbm, v_ref, sems.at[1])
-    k_copy.start()
-    v_copy.start()
-
-    tile_ids = [(2 * (j // 2) + at.core) * 4 + half * 2 + j % 2 for j in range(4)]
+    spots = [at.partner(dy, dz) for dy, dz in offsets]
+    tile_ids = [(2 * y + at.core) * 4 + z for y, z in spots]
     homes = [leaf_tiles[a] for a in tile_ids]
-    for j in range(4):
+    tiles = range(len(offsets))
+    for j in tiles:
         visits[j, 0] = homes[j]
 
     def look(t, counts):
         after = []
-        for j in range(4):
+        for j in tiles:
             visits[j, counts[j]] = t
             hit = jnp.logical_and(ancestry[tile_ids[j], t] == 1, t != homes[j])
             after.append(counts[j] + jnp.where(hit, 1, 0))
         return tuple(after)
 
-    counts = lax.fori_loop(0, ancestry.shape[1], look, (jnp.int32(1),) * 4)
-    for j in range(4):
+    counts = lax.fori_loop(
+        0, ancestry.shape[1], look, (jnp.int32(1),) * len(offsets), unroll=8
+    )
+    for j in tiles:
         visits[j, counts[j]] = 0
-
-    k_copy.wait()
-    v_copy.wait()
 
     def pair_of(ref, j, i):
         first = ref[aligned(visits[j, 2 * i], TILE), :]
         second = ref[aligned(visits[j, 2 * i + 1], TILE), :]
         return jnp.concatenate([first, second], axis=0)
 
-    for j in range(4):
-        rows = pl.ds(j * TILE, TILE)
+    for j in tiles:
+        rows = aligned(head_of(*spots[j]), TILE)
         query = jnp.concatenate(
             [q_ref[rows, pl.ds(g * DH, DH)] for g in range(GROUP)], axis=0
         )
@@ -279,48 +273,42 @@
 
         result = sum_ref[...] / jnp.sum(total_ref[...], axis=1, keepdims=True)
         for g in range(GROUP):
-            out_ref[rows, pl.ds(g * DH, DH)] = result[g * TILE : (g + 1) * TILE].astype(
+            outs[j][:, pl.ds(g * DH, DH)] = result[g * TILE : (g + 1) * TILE].astype(
                 jnp.bfloat16
             )
 
 
-def return_kernel(part_ref, out_ref, send_sem, recv_sem, own_sem):
+def assemble_kernel(*refs):
+    pieces, out_ref, sems = refs[:4], refs[4], refs[5]
     at = Place()
-    head = head_of(at.y, at.z)
-    partners = [at.partner(dy, dz) for dy, dz in GROUP_OFFSETS]
-    greet([at.device(y, at.core, z) for y, z in partners])
-    own = pltpu.make_async_copy(
-        part_ref.at[aligned(head, TILE)], out_ref.at[:, aligned(head, WIDE)], own_sem
-    )
-    sends, arrivals = [], []
-    for i, (y, z) in enumerate(partners):
-        there = head_of(y, z)
-        common = dict(
-            src_ref=part_ref.at[aligned(there, TILE)],
-            send_sem=send_sem.at[i],
-            recv_sem=recv_sem.at[i],
-            device_id=at.device(y, at.core, z),
-            device_id_type=MESH,
-        )
-        sends.append(
-            pltpu.make_async_remote_copy(dst_ref=out_ref.at[:, aligned(head, WIDE)], **common)
-        )
-        arrivals.append(
-            pltpu.make_async_remote_copy(dst_ref=out_ref.at[:, aligned(there, WIDE)], **common)
-        )
-    for copy in sends:
+    copies = []
+    for i, offset in enumerate(((0, 0),) + GROUP_OFFSETS):
+        head = head_of(*at.partner(*offset))
+        copies.append(
+            pltpu.make_async_copy(
+                pieces[i], out_ref.at[:, aligned(head, WIDE)], sems.at[i]
+            )
+        )
+    for copy in copies:
         copy.start()
-    own.start()
-    own.wait()
-    for copy in arrivals:
-        copy.wait_recv()
-    for copy in sends:
-        copy.wait_send()
+    for copy in copies:
+        copy.wait()
+
+
+def pairs_of(dy, dz):
+    pairs = []
+    for blk in range(4):
+        for z in range(4):
+            y, core = blk // 2, blk % 2
+            there = z + 1 - 2 * (z % 2) if dz else z
+            pairs.append((blk * 4 + z, (2 * (y ^ dy) + core) * 4 + there))
+    return pairs
 
 
 def on_device(group_size, queries, keys, values, ancestry, leaf_tiles):
     rows = queries.shape[0]
     total_keys = keys.shape[0] * group_size
+    hbm = pl.BlockSpec(memory_space=pltpu.HBM)
     any_space = pl.BlockSpec(memory_space=pl.ANY)
     vmem = pl.BlockSpec(memory_space=pltpu.VMEM)
     smem = pl.BlockSpec(memory_space=pltpu.SMEM)
@@ -334,45 +322,59 @@
             jax.ShapeDtypeStruct((total_keys, DH), bf16),
             jax.ShapeDtypeStruct((total_keys, DH), bf16),
         ),
-        in_specs=[any_space] * 3,
-        out_specs=[any_space] * 3,
+        in_specs=[hbm] * 3,
+        out_specs=[vmem] * 3,
         scratch_shapes=[
             dma((2 * n,)), dma((2 * n,)), dma((2 * n + 2,)), dma((2 * n + 2,)),
             dma((3,)), dma((3,)), dma((3,)),
         ],
-        compiler_params=pltpu.CompilerParams(collective_id=0, has_side_effects=True),
+        compiler_params=pltpu.CompilerParams(
+            collective_id=0, has_side_effects=True, vmem_limit_bytes=59 * 1024 * 1024
+        ),
         name="gather_heads",
     )(queries, keys, values)
 
     tiles = total_keys // TILE
-    part = pl.pallas_call(
-        attend_kernel,
-        out_shape=jax.ShapeDtypeStruct((4 * rows, WIDE), bf16),
-        in_specs=[smem, smem, vmem, any_space, any_space],
-        out_specs=vmem,
-        scratch_shapes=[
-            pltpu.VMEM((total_keys, DH), bf16),
-            pltpu.VMEM((total_keys, DH), bf16),
-            pltpu.VMEM((tiles // 2, WIDE, 2 * TILE), jnp.float32),
-            pltpu.VMEM((WIDE, TILE), jnp.float32),
-            pltpu.VMEM((WIDE, TILE), jnp.float32),
-            pltpu.VMEM((WIDE, DH), jnp.float32),
-            pltpu.SMEM((4, 128), jnp.int32),
-            dma((2,)),
-        ],
-        compiler_params=pltpu.CompilerParams(vmem_limit_bytes=48 * 1024 * 1024),
-        name="attend_tree",
-    )(ancestry, leaf_tiles, q_all, k_all, v_all)
+
+    def attend(offsets, name):
+        piece = jax.ShapeDtypeStruct((rows, WIDE), bf16)
+        work = len(offsets) * 16 * WIDE * TILE * DH * 4
+        return pl.pallas_call(
+            functools.partial(attend_kernel, offsets),
+            out_shape=(piece,) * len(offsets),
+            in_specs=[smem, smem, vmem, vmem, vmem],
+            out_specs=(vmem,) * len(offsets),
+            scratch_shapes=[
+                pltpu.VMEM((tiles // 2, WIDE, 2 * TILE), jnp.float32),
+                pltpu.VMEM((WIDE, TILE), jnp.float32),
+                pltpu.VMEM((WIDE, TILE), jnp.float32),
+                pltpu.VMEM((WIDE, DH), jnp.float32),
+                pltpu.SMEM((4, 128), jnp.int32),
+            ],
+            compiler_params=pltpu.CompilerParams(vmem_limit_bytes=40 * 1024 * 1024),
+            cost_estimate=pl.CostEstimate(
+                flops=work, bytes_accessed=4 * total_keys * DH, transcendentals=0
+            ),
+            name=name,
+        )(ancestry, leaf_tiles, q_all, k_all, v_all)
+
+    def send(piece, offset):
+        return lax.ppermute(piece, ("blk", "kv"), pairs_of(*offset))
+
+    far = attend(GROUP_OFFSETS[:2], "attend_far")
+    arrived = [send(piece, offset) for piece, offset in zip(far, GROUP_OFFSETS)]
+    (near,) = attend(GROUP_OFFSETS[2:], "attend_near")
+    arrived.append(send(near, GROUP_OFFSETS[2]))
+    (own,) = attend(((0, 0),), "attend_own")
 
     return pl.pallas_call(
-        return_kernel,
+        assemble_kernel,
         out_shape=jax.ShapeDtypeStruct((rows, KV_HEADS * WIDE), bf16),
-        in_specs=[any_space],
+        in_specs=[any_space] * 4,
         out_specs=any_space,
-        scratch_shapes=[dma((3,)), dma((3,)), dma],
-        compiler_params=pltpu.CompilerParams(collective_id=1, has_side_effects=True),
-        name="return_heads",
-    )(part)
+        scratch_shapes=[dma((4,))],
+        name="assemble_heads",
+    )(own, *arrived)
 
 
 def solution(mesh):

time: 85 us -> 104 us (1.22)
  Pallas kernels: 76.3 us -> 88.2 us
  waiting for transfers between devices: 0 us -> 4.3 us
  starting transfers between devices: 0 us -> 3.43 us
  local copies, waits for them, and re-layouts: 8.41 us -> 6.93 us
    pallas_call x2 -> x4, Pallas kernels: 19.8 us -> 30 us  [the longest x1 21 us: on_device(): pl.pallas_call(assemble_kernel, out_shape=jax.ShapeDtypeStruct((rows, KV_...]
    ppermute x0 -> x3, waiting for transfers between devices: none -> 4.3 us  [send(): return lax.ppermute(piece, ('blk', 'kv'), pairs_of(*offset))]
    ppermute x0 -> x3, starting transfers between devices: none -> 3.43 us  [send(): return lax.ppermute(piece, ('blk', 'kv'), pairs_of(*offset))]
    pallas_call x1, Pallas kernels: 56.5 us -> 58.2 us  [on_device(): pl.pallas_call(gather_kernel, out_shape=(jax.ShapeDtypeStruct((4 * rows,...]
    unnamed x13 -> x18, local copies, waits for them, and re-layouts: 8.41 us -> 6.93 us
  transfers between devices with their start and end apart: 0 -> 3, of which waited for: 0 -> 2; matrix products, arithmetic and copies ran while one was open for 0% -> 0% of each run, Pallas kernels for 0% -> 4%
where the time goes in v3:
time: 104 us; the launch traced here: 103 us
  Pallas kernels  88.2 us (85%)
  local copies, waits for them, and re-layouts  6.93 us (7%)
  waiting for transfers between devices  4.3 us (4%)
  starting transfers between devices  3.43 us (3%)
    pallas_call x1, Pallas kernels, on_device(): pl.pallas_call(gather_kernel, out_shape=(jax.ShapeDtypeStruct((4 * rows,...  58.2 us
    pallas_call x1, Pallas kernels, on_device(): pl.pallas_call(assemble_kernel, out_shape=jax.ShapeDtypeStruct((rows, KV_...  21 us
    pallas_call x3, Pallas kernels, attend(): pl.pallas_call(functools.partial(attend_kernel, offsets), out_shape=(piec...  9.06 us
    unnamed x18, local copies, waits for them, and re-layouts  6.93 us
    ppermute x3, waiting for transfers between devices, send(): return lax.ppermute(piece, ('blk', 'kv'), pairs_of(*offset))  4.3 us
    ppermute x3, starting transfers between devices, send(): return lax.ppermute(piece, ('blk', 'kv'), pairs_of(*offset))  3.43 us
  transfers between devices with their start and end apart: 3, of which 2 were waited for; matrix products, arithmetic and copies ran while one was open for 0% of the time, Pallas kernels for 4%

profile of v3, /device:TPU:0, one launch (start us, length us, event | category | flops | bytes accessed | tf_op | source)
XLA Modules:
  0.0 103.0 jit_solution(15494607798988352462)
XLA Ops:
  0.0 58.2 %gather_heads.1 = (bf16[512,640]{1,0:T(8,128)(2,1)}, bf16[8192,128]{1,0:T(8,128)(2,1)}, bf16[8192,128]{1,0:T(8,128)(2,1)}) custom-call(bf16[128,2560]{1,0:T(8,128)(2,1)} %q_ref.1, bf16[512,512]{1,0:T(8,128)(2,1)} %k_ref.1, bf16[512,512]{1,0:T(8,128)(2,1)} %v_ref.1), custom_call_target="tpu_custom_call" | custom-call | tf_op jit(solution)/shard_map/gather_heads/pallas_call | solution.py:318
  58.2 0.0 copy-start
  58.2 1.6 %copy-done = bf16[8192,128]{1,0:T(8,128)(2,1)S(1)} copy-done((bf16[8192,128]{1,0:T(8,128)(2,1)S(1)}, bf16[8192,128]{1,0:T(8,128)(2,1)}, u32[]{:S(2)}) %copy-start) | copy-done | bytes 2097176
  59.8 0.0 copy-start.1
  59.8 1.6 %copy-done.1 = bf16[8192,128]{1,0:T(8,128)(2,1)S(1)} copy-done((bf16[8192,128]{1,0:T(8,128)(2,1)S(1)}, bf16[8192,128]{1,0:T(8,128)(2,1)}, u32[]{:S(2)}) %copy-start.1) | copy-done | bytes 2097176
  61.4 0.0 copy-start.2
  61.4 1.1 %copy-done.2 = bf16[512,640]{1,0:T(8,128)(2,1)S(1)} copy-done((bf16[512,640]{1,0:T(8,128)(2,1)S(1)}, bf16[512,640]{1,0:T(8,128)(2,1)}, u32[]{:S(2)}) %copy-start.2) | copy-done | bytes 655384
  62.5 0.7 copy-done.4
  63.2 0.7 copy-done.5
  63.8 5.1 %attend_far.1 = (bf16[128,640]{1,0:T(8,128)(2,1)S(1)}, bf16[128,640]{1,0:T(8,128)(2,1)S(1)}) custom-call(s32[16,64]{1,0:T(8,128)S(1)} %copy-done.4, s32[16]{0:T(128)S(1)} %copy-done.5, bf16[512,640]{1,0:T(8,128)(2,1)S(1)} %copy-done.2, bf16[8192,128]{1,0:T(8,128)(2,1)S(1)} %copy-done, bf16[8192,128]{1,0:T(8,128)(2,1)S(1)} %copy-done.1), custom_call_target="tpu_custom_call" | custom-call | flops 1342177280 | bytes 4194304 | tf_op jit(solution)/shard_map/attend_far/pallas_call | solution.py:342
  69.0 0.1 collective-permute-start
  69.0 3.3 %collective-permute-start.1 = (bf16[128,640]{1,0:T(8,128)(2,1)S(1)}, bf16[128,640]{1,0:T(8,128)(2,1)S(1)}, u32[]{:S(2)}, u32[]{:S(2)}) collective-permute-start(bf16[128,640]{1,0:T(8,128)(2,1)S(1)} %get-tuple-element.14), channel_id=1, source_target_pairs={{0,1},{1,0},{2,3},{3,2},{4,5},{5,4},{6,7},{7,6},{8,9},{9,8},{10,11... | collective-permute-start | bytes 491528 | tf_op jit(solution)/shard_map/ppermute | solution.py:362
  72.3 2.2 %attend_near.1 = bf16[128,640]{1,0:T(8,128)(2,1)S(1)} custom-call(s32[16,64]{1,0:T(8,128)S(1)} %copy-done.4, s32[16]{0:T(128)S(1)} %copy-done.5, bf16[512,640]{1,0:T(8,128)(2,1)S(1)} %copy-done.2, bf16[8192,128]{1,0:T(8,128)(2,1)S(1)} %copy-done, bf16[8192,128]{1,0:T(8,128)(2,1)S(1)} %copy-done.1), custom_call_target="tpu_custom_call" | custom-call | flops 671088640 | bytes 4194304 | tf_op jit(solution)/shard_map/attend_near/pallas_call | solution.py:342
  74.6 0.1 collective-permute-start.2
  74.6 1.7 %attend_own.1.refs_0_ = bf16[128,640]{1,0:T(8,128)(2,1)S(1)} custom-call(s32[16,64]{1,0:T(8,128)S(1)} %copy-done.4, s32[16]{0:T(128)S(1)} %copy-done.5, bf16[512,640]{1,0:T(8,128)(2,1)S(1)} %copy-done.2, bf16[8192,128]{1,0:T(8,128)(2,1)S(1)} %copy-done, bf16[8192,128]{1,0:T(8,128)(2,1)S(1)} %copy-done.1), custom_call_target="tpu_custom_call" | custom-call | flops 671088640 | bytes 4194304 | tf_op jit(solution)/shard_map/attend_own/pallas_call | solution.py:342
  76.3 0.0 copy-start.3
  76.4 0.7 copy-done.3
  77.0 0.0 collective-permute-done.refs_1_
  77.0 3.5 %collective-permute-done.1.refs_2_ = bf16[128,640]{1,0:T(8,128)(2,1)S(1)} collective-permute-done((bf16[128,640]{1,0:T(8,128)(2,1)S(1)}, bf16[128,640]{1,0:T(8,128)(2,1)S(1)}, u32[]{:S(2)}, u32[]{:S(2)}) %collective-permute-start.1) | collective-permute-done | bytes 163872 | tf_op jit(solution)/shard_map/ppermute | solution.py:362
  80.5 0.8 collective-permute-done.2.refs_3_
  81.3 0.0 copy-done.6
  81.3 0.0 copy-done.7
  81.3 0.7 copy-done.8
  82.0 21.0 %assemble_heads.1 = bf16[128,2560]{1,0:T(8,128)(2,1)} custom-call(bf16[128,640]{1,0:T(8,128)(2,1)} %copy-done.3, bf16[128,640]{1,0:T(8,128)(2,1)} %copy-done.6, bf16[128,640]{1,0:T(8,128)(2,1)} %copy-done.7, bf16[128,640]{1,0:T(8,128)(2,1)} %copy-done.8), custom_call_target="tpu_custom_call" | custom-call | tf_op jit(solution)/shard_map/assemble_heads/pallas_call | solution.py:370
  (5 shorter events, 0.0 us)
Async XLA Ops:
  58.2 1.6 %copy-start = (bf16[8192,128]{1,0:T(8,128)(2,1)S(1)}, bf16[8192,128]{1,0:T(8,128)(2,1)}, u32[]{:S(2)}) copy-start(bf16[8192,128]{1,0:T(8,128)(2,1)} %get-tuple-element.11.k_ref) | copy-start | bytes 6291460
  59.8 1.6 %copy-start.1 = (bf16[8192,128]{1,0:T(8,128)(2,1)S(1)}, bf16[8192,128]{1,0:T(8,128)(2,1)}, u32[]{:S(2)}) copy-start(bf16[8192,128]{1,0:T(8,128)(2,1)} %get-tuple-element.12.v_ref) | copy-start | bytes 6291460
  61.4 1.1 %copy-start.2 = (bf16[512,640]{1,0:T(8,128)(2,1)S(1)}, bf16[512,640]{1,0:T(8,128)(2,1)}, u32[]{:S(2)}) copy-start(bf16[512,640]{1,0:T(8,128)(2,1)} %get-tuple-element.10.q_ref) | copy-start | bytes 1966084
  62.5 0.7 copy-start.4
  63.2 0.7 copy-start.5
  69.0 8.1 %collective-permute-start = (bf16[128,640]{1,0:T(8,128)(2,1)S(1)}, bf16[128,640]{1,0:T(8,128)(2,1)S(1)}, u32[]{:S(2)}, u32[]{:S(2)}) collective-permute-start(bf16[128,640]{1,0:T(8,128)(2,1)S(1)} %get-tuple-element.13), channel_id=1, source_target_pairs={{0,9},{1,8},{2,11},{3,10},{4,13},{5,12},{6,15},{7,14},{8,1},{9,0},... | collective-permute-start | bytes 491528 | tf_op jit(solution)/shard_map/ppermute | solution.py:362
  69.0 11.4 %collective-permute-start.1 = (bf16[128,640]{1,0:T(8,128)(2,1)S(1)}, bf16[128,640]{1,0:T(8,128)(2,1)S(1)}, u32[]{:S(2)}, u32[]{:S(2)}) collective-permute-start(bf16[128,640]{1,0:T(8,128)(2,1)S(1)} %get-tuple-element.14), channel_id=1, source_target_pairs={{0,1},{1,0},{2,3},{3,2},{4,5},{5,4},{6,7},{7,6},{8,9},{9,8},{10,11... | collective-permute-start | bytes 491528 | tf_op jit(solution)/shard_map/ppermute | solution.py:362
  74.6 6.8 %collective-permute-start.2 = (bf16[128,640]{1,0:T(8,128)(2,1)S(1)}, bf16[128,640]{1,0:T(8,128)(2,1)S(1)}, u32[]{:S(2)}, u32[]{:S(2)}) collective-permute-start(bf16[128,640]{1,0:T(8,128)(2,1)S(1)} %attend_near.1), channel_id=1, source_target_pairs={{0,8},{1,9},{2,10},{3,11},{4,12},{5,13},{6,14},{7,15},{8,0},{9,1},... | collective-permute-start | bytes 491528 | tf_op jit(solution)/shard_map/ppermute | solution.py:362
  76.3 0.7 copy-start.3
  77.0 4.3 %copy-start.6 = (bf16[128,640]{1,0:T(8,128)(2,1)}, bf16[128,640]{1,0:T(8,128)(2,1)S(1)}, u32[]{:S(2)}) copy-start(bf16[128,640]{1,0:T(8,128)(2,1)S(1)} %collective-permute-done.refs_1_) | copy-start | bytes 491524
  80.5 0.8 copy-start.7
  81.3 0.7 copy-start.8

commit v4 on v3

--- a/solution.py
+++ b/solution.py
@@ -279,20 +279,11 @@
 
 
 def assemble_kernel(*refs):
-    pieces, out_ref, sems = refs[:4], refs[4], refs[5]
+    pieces, out_ref = refs[:4], refs[4]
     at = Place()
-    copies = []
     for i, offset in enumerate(((0, 0),) + GROUP_OFFSETS):
         head = head_of(*at.partner(*offset))
-        copies.append(
-            pltpu.make_async_copy(
-                pieces[i], out_ref.at[:, aligned(head, WIDE)], sems.at[i]
-            )
-        )
-    for copy in copies:
-        copy.start()
-    for copy in copies:
-        copy.wait()
+        out_ref[:, aligned(head, WIDE)] = pieces[i][...]
 
 
 def pairs_of(dy, dz):
@@ -309,7 +300,6 @@
     rows = queries.shape[0]
     total_keys = keys.shape[0] * group_size
     hbm = pl.BlockSpec(memory_space=pltpu.HBM)
-    any_space = pl.BlockSpec(memory_space=pl.ANY)
     vmem = pl.BlockSpec(memory_space=pltpu.VMEM)
     smem = pl.BlockSpec(memory_space=pltpu.SMEM)
     dma = pltpu.SemaphoreType.DMA
@@ -329,7 +319,7 @@
             dma((3,)), dma((3,)), dma((3,)),
         ],
         compiler_params=pltpu.CompilerParams(
-            collective_id=0, has_side_effects=True, vmem_limit_bytes=59 * 1024 * 1024
+            collective_id=0, has_side_effects=True, vmem_limit_bytes=16 * 1024 * 1024
         ),
         name="gather_heads",
     )(queries, keys, values)
@@ -370,9 +360,8 @@
     return pl.pallas_call(
         assemble_kernel,
         out_shape=jax.ShapeDtypeStruct((rows, KV_HEADS * WIDE), bf16),
-        in_specs=[any_space] * 4,
-        out_specs=any_space,
-        scratch_shapes=[dma((4,))],
+        in_specs=[vmem] * 4,
+        out_specs=vmem,
         name="assemble_heads",
     )(own, *arrived)
 

time: 104 us -> 81.1 us (0.78)
  Pallas kernels: 88.2 us -> 67 us
  local copies, waits for them, and re-layouts: 6.93 us -> 5.84 us
    pallas_call x1, Pallas kernels: 21 us -> 2.06 us  [on_device(): pl.pallas_call(assemble_kernel, out_shape=jax.ShapeDtypeStruct((rows, KV_...]
    pallas_call x1, Pallas kernels: 58.2 us -> 55.8 us  [on_device(): pl.pallas_call(gather_kernel, out_shape=(jax.ShapeDtypeStruct((4 * rows,...]
    unnamed x18, local copies, waits for them, and re-layouts: 6.93 us -> 5.84 us
  transfers between devices with their start and end apart: 3 -> 3, of which waited for: 2 -> 2; matrix products, arithmetic and copies ran while one was open for 0% -> 0% of each run, Pallas kernels for 4% -> 6%
where the time goes in v4:
time: 81.1 us; the launch traced here: 80.4 us
  Pallas kernels  67 us (83%)
  local copies, waits for them, and re-layouts  5.84 us (7%)
  waiting for transfers between devices  4.09 us (5%)
  starting transfers between devices  3.41 us (4%)
    pallas_call x1, Pallas kernels, on_device(): pl.pallas_call(gather_kernel, out_shape=(jax.ShapeDtypeStruct((4 * rows,...  55.8 us
    pallas_call x3, Pallas kernels, attend(): pl.pallas_call(functools.partial(attend_kernel, offsets), out_shape=(piec...  9.08 us
    unnamed x18, local copies, waits for them, and re-layouts  5.84 us
    ppermute x3, waiting for transfers between devices, send(): return lax.ppermute(piece, ('blk', 'kv'), pairs_of(*offset))  4.09 us
    ppermute x3, starting transfers between devices, send(): return lax.ppermute(piece, ('blk', 'kv'), pairs_of(*offset))  3.41 us
    pallas_call x1, Pallas kernels, on_device(): pl.pallas_call(assemble_kernel, out_shape=jax.ShapeDtypeStruct((rows, KV_...  2.06 us
  transfers between devices with their start and end apart: 3, of which 2 were waited for; matrix products, arithmetic and copies ran while one was open for 0% of the time, Pallas kernels for 6%

profile of v4, /device:TPU:0, one launch (start us, length us, event | category | flops | bytes accessed | tf_op | source)
XLA Modules:
  0.0 80.4 jit_solution(4354626101211425771)
XLA Ops:
  0.0 0.0 copy-start
  0.0 1.1 %copy-done = bf16[128,2560]{1,0:T(8,128)(2,1)S(1)} copy-done((bf16[128,2560]{1,0:T(8,128)(2,1)S(1)}, bf16[128,2560]{1,0:T(8,128)(2,1)}, u32[]{:S(2)}) %copy-start) | copy-done | bytes 655384
  1.1 0.0 copy-start.2
  1.1 1.0 %copy-done.2 = bf16[512,512]{1,0:T(8,128)(2,1)S(1)} copy-done((bf16[512,512]{1,0:T(8,128)(2,1)S(1)}, bf16[512,512]{1,0:T(8,128)(2,1)}, u32[]{:S(2)}) %copy-start.2) | copy-done | bytes 524312
  2.1 1.0 %copy-done.3 = bf16[512,512]{1,0:T(8,128)(2,1)S(1)} copy-done((bf16[512,512]{1,0:T(8,128)(2,1)S(1)}, bf16[512,512]{1,0:T(8,128)(2,1)}, u32[]{:S(2)}) %copy-start.3) | copy-done | bytes 524312
  3.2 55.8 %gather_heads.1 = (bf16[512,640]{1,0:T(8,128)(2,1)S(1)}, bf16[8192,128]{1,0:T(8,128)(2,1)S(1)}, bf16[8192,128]{1,0:T(8,128)(2,1)S(1)}) custom-call(bf16[128,2560]{1,0:T(8,128)(2,1)S(1)} %copy-done, bf16[512,512]{1,0:T(8,128)(2,1)S(1)} %copy-done.2, bf16[512,512]{1,0:T(8,128)(2,1)S(1)} %copy-done.3), custom_call_target="tpu_custom_call" | custom-call | tf_op jit(solution)/shard_map/gather_heads/pallas_call | solution.py:308
  59.0 0.0 copy-start.4
  59.0 0.7 copy-done.4
  59.7 0.7 copy-done.5
  60.4 4.1 %attend_far.1 = (bf16[128,640]{1,0:T(8,128)(2,1)S(1)}, bf16[128,640]{1,0:T(8,128)(2,1)S(1)}) custom-call(s32[16,64]{1,0:T(8,128)S(1)} %copy-done.4, s32[16]{0:T(128)S(1)} %copy-done.5, bf16[512,640]{1,0:T(8,128)(2,1)S(1)} %get-tuple-element.10.q_ref, bf16[8192,128]{1,0:T(8,128)(2,1)S(1)} %get-tuple-element.11.k_ref, ...), custom_call_target="tpu_custom_call" | custom-call | flops 1342177280 | bytes 4194304 | tf_op jit(solution)/shard_map/attend_far/pallas_call | solution.py:332
  64.5 0.1 collective-permute-start
  64.6 3.3 %collective-permute-start.1 = (bf16[128,640]{1,0:T(8,128)(2,1)S(1)}, bf16[128,640]{1,0:T(8,128)(2,1)S(1)}, u32[]{:S(2)}, u32[]{:S(2)}) collective-permute-start(bf16[128,640]{1,0:T(8,128)(2,1)S(1)} %get-tuple-element.14), channel_id=1, source_target_pairs={{0,1},{1,0},{2,3},{3,2},{4,5},{5,4},{6,7},{7,6},{8,9},{9,8},{10,11... | collective-permute-start | bytes 491528 | tf_op jit(solution)/shard_map/ppermute | solution.py:352
  67.8 2.7 %attend_near.1 = bf16[128,640]{1,0:T(8,128)(2,1)S(1)} custom-call(s32[16,64]{1,0:T(8,128)S(1)} %copy-done.4, s32[16]{0:T(128)S(1)} %copy-done.5, bf16[512,640]{1,0:T(8,128)(2,1)S(1)} %get-tuple-element.10.q_ref, bf16[8192,128]{1,0:T(8,128)(2,1)S(1)} %get-tuple-element.11.k_ref, bf16[8192,128]{1,0:T(8,128)(2,1)S(1)} %get-tuple-element.12.v_ref), custom_call_target="tpu_custom_call" | custom-call | flops 671088640 | bytes 4194304 | tf_op jit(solution)/shard_map/attend_near/pallas_call | solution.py:332
  70.6 0.1 collective-permute-start.2
  70.7 2.2 %attend_own.1.refs_0_ = bf16[128,640]{1,0:T(8,128)(2,1)S(1)} custom-call(s32[16,64]{1,0:T(8,128)S(1)} %copy-done.4, s32[16]{0:T(128)S(1)} %copy-done.5, bf16[512,640]{1,0:T(8,128)(2,1)S(1)} %get-tuple-element.10.q_ref, bf16[8192,128]{1,0:T(8,128)(2,1)S(1)} %get-tuple-element.11.k_ref, bf16[8192,128]{1,0:T(8,128)(2,1)S(1)} %get-tuple-element.12.v_ref), custom_call_target="tpu_custom_call" | custom-call | flops 671088640 | bytes 4194304 | tf_op jit(solution)/shard_map/attend_own/pallas_call | solution.py:332
  72.9 0.0 copy-start.1
  72.9 0.7 copy-done.1
  73.6 0.0 collective-permute-done.refs_1_
  73.6 2.8 %collective-permute-done.1.refs_2_ = bf16[128,640]{1,0:T(8,128)(2,1)S(1)} collective-permute-done((bf16[128,640]{1,0:T(8,128)(2,1)S(1)}, bf16[128,640]{1,0:T(8,128)(2,1)S(1)}, u32[]{:S(2)}, u32[]{:S(2)}) %collective-permute-start.1) | collective-permute-done | bytes 163872 | tf_op jit(solution)/shard_map/ppermute | solution.py:352
  76.4 1.3 %collective-permute-done.2.refs_3_ = bf16[128,640]{1,0:T(8,128)(2,1)S(1)} collective-permute-done((bf16[128,640]{1,0:T(8,128)(2,1)S(1)}, bf16[128,640]{1,0:T(8,128)(2,1)S(1)}, u32[]{:S(2)}, u32[]{:S(2)}) %collective-permute-start.2) | collective-permute-done | bytes 163872 | tf_op jit(solution)/shard_map/ppermute | solution.py:352
  77.7 0.0 copy-done.6
  77.7 0.0 copy-done.7
  77.7 0.7 copy-done.8
  78.3 2.1 %assemble_heads.1 = bf16[128,2560]{1,0:T(8,128)(2,1)} custom-call(bf16[128,640]{1,0:T(8,128)(2,1)} %copy-done.1, bf16[128,640]{1,0:T(8,128)(2,1)} %copy-done.6, bf16[128,640]{1,0:T(8,128)(2,1)} %copy-done.7, bf16[128,640]{1,0:T(8,128)(2,1)} %copy-done.8), custom_call_target="tpu_custom_call" | custom-call | tf_op jit(solution)/shard_map/assemble_heads/pallas_call | solution.py:360
  (5 shorter events, 0.0 us)
Async XLA Ops:
  0.0 1.1 %copy-start = (bf16[128,2560]{1,0:T(8,128)(2,1)S(1)}, bf16[128,2560]{1,0:T(8,128)(2,1)}, u32[]{:S(2)}) copy-start(bf16[128,2560]{1,0:T(8,128)(2,1)} %q_ref.1) | copy-start | bytes 1966084
  1.1 1.0 %copy-start.2 = (bf16[512,512]{1,0:T(8,128)(2,1)S(1)}, bf16[512,512]{1,0:T(8,128)(2,1)}, u32[]{:S(2)}) copy-start(bf16[512,512]{1,0:T(8,128)(2,1)} %k_ref.1) | copy-start | bytes 1572868
  2.1 1.0 %copy-start.3 = (bf16[512,512]{1,0:T(8,128)(2,1)S(1)}, bf16[512,512]{1,0:T(8,128)(2,1)}, u32[]{:S(2)}) copy-start(bf16[512,512]{1,0:T(8,128)(2,1)} %v_ref.1) | copy-start | bytes 1572868
  59.0 0.7 copy-start.4
  59.7 0.7 copy-start.5
  64.5 9.1 %collective-permute-start = (bf16[128,640]{1,0:T(8,128)(2,1)S(1)}, bf16[128,640]{1,0:T(8,128)(2,1)S(1)}, u32[]{:S(2)}, u32[]{:S(2)}) collective-permute-start(bf16[128,640]{1,0:T(8,128)(2,1)S(1)} %get-tuple-element.13), channel_id=1, source_target_pairs={{0,9},{1,8},{2,11},{3,10},{4,13},{5,12},{6,15},{7,14},{8,1},{9,0},... | collective-permute-start | bytes 491528 | tf_op jit(solution)/shard_map/ppermute | solution.py:352
  64.6 11.8 %collective-permute-start.1 = (bf16[128,640]{1,0:T(8,128)(2,1)S(1)}, bf16[128,640]{1,0:T(8,128)(2,1)S(1)}, u32[]{:S(2)}, u32[]{:S(2)}) collective-permute-start(bf16[128,640]{1,0:T(8,128)(2,1)S(1)} %get-tuple-element.14), channel_id=1, source_target_pairs={{0,1},{1,0},{2,3},{3,2},{4,5},{5,4},{6,7},{7,6},{8,9},{9,8},{10,11... | collective-permute-start | bytes 491528 | tf_op jit(solution)/shard_map/ppermute | solution.py:352
  70.6 7.1 %collective-permute-start.2 = (bf16[128,640]{1,0:T(8,128)(2,1)S(1)}, bf16[128,640]{1,0:T(8,128)(2,1)S(1)}, u32[]{:S(2)}, u32[]{:S(2)}) collective-permute-start(bf16[128,640]{1,0:T(8,128)(2,1)S(1)} %attend_near.1), channel_id=1, source_target_pairs={{0,8},{1,9},{2,10},{3,11},{4,12},{5,13},{6,14},{7,15},{8,0},{9,1},... | collective-permute-start | bytes 491528 | tf_op jit(solution)/shard_map/ppermute | solution.py:352
  72.9 0.7 copy-start.1
  73.6 4.1 %copy-start.6 = (bf16[128,640]{1,0:T(8,128)(2,1)}, bf16[128,640]{1,0:T(8,128)(2,1)S(1)}, u32[]{:S(2)}) copy-start(bf16[128,640]{1,0:T(8,128)(2,1)S(1)} %collective-permute-done.refs_1_) | copy-start | bytes 491524
  76.4 1.3 %copy-start.7 = (bf16[128,640]{1,0:T(8,128)(2,1)}, bf16[128,640]{1,0:T(8,128)(2,1)S(1)}, u32[]{:S(2)}) copy-start(bf16[128,640]{1,0:T(8,128)(2,1)S(1)} %collective-permute-done.1.refs_2_) | copy-start | bytes 491524
  77.7 0.7 copy-start.8

commit v5 on v4

--- a/solution.py
+++ b/solution.py
@@ -60,7 +60,8 @@
 
 
 def gather_kernel(
-    q_ref, k_ref, v_ref, q_all, k_all, v_all,
+    q_ref, k_ref, v_ref, ancestry, leaf_tiles,
+    q_all, k_all, v_all, ancestry_out, leaf_tiles_out,
     kv_send, kv_recv, pass_send, pass_recv, q_send, q_recv, own_sem,
 ):
     at = Place()
@@ -162,7 +163,9 @@
     ] + [
         pltpu.make_async_copy(
             q_ref.at[:, aligned(head, WIDE)], q_all.at[aligned(head, TILE)], own_sem.at[2]
-        )
+        ),
+        pltpu.make_async_copy(ancestry, ancestry_out, own_sem.at[3]),
+        pltpu.make_async_copy(leaf_tiles, leaf_tiles_out, own_sem.at[4]),
     ]
     for copy in locals_:
         copy.start()
@@ -305,24 +308,30 @@
     dma = pltpu.SemaphoreType.DMA
     bf16 = jnp.bfloat16
     n = len(KV_OFFSETS)
-    q_all, k_all, v_all = pl.pallas_call(
+    arguments = [
+        pltpu.with_memory_space_constraint(x, pltpu.HBM)
+        for x in (queries, keys, values, ancestry, leaf_tiles)
+    ]
+    q_all, k_all, v_all, ancestry, leaf_tiles = pl.pallas_call(
         gather_kernel,
         out_shape=(
             jax.ShapeDtypeStruct((4 * rows, WIDE), bf16),
             jax.ShapeDtypeStruct((total_keys, DH), bf16),
             jax.ShapeDtypeStruct((total_keys, DH), bf16),
+            jax.ShapeDtypeStruct(ancestry.shape, ancestry.dtype),
+            jax.ShapeDtypeStruct(leaf_tiles.shape, leaf_tiles.dtype),
         ),
-        in_specs=[hbm] * 3,
-        out_specs=[vmem] * 3,
+        in_specs=[hbm] * 5,
+        out_specs=[vmem] * 5,
         scratch_shapes=[
             dma((2 * n,)), dma((2 * n,)), dma((2 * n + 2,)), dma((2 * n + 2,)),
-            dma((3,)), dma((3,)), dma((3,)),
+            dma((3,)), dma((3,)), dma((5,)),
         ],
         compiler_params=pltpu.CompilerParams(
             collective_id=0, has_side_effects=True, vmem_limit_bytes=16 * 1024 * 1024
         ),
         name="gather_heads",
-    )(queries, keys, values)
+    )(*arguments)
 
     tiles = total_keys // TILE
 

time: 81.1 us -> 76.2 us (0.940); the launches traced: 80.4 us -> 76.6 us
  local copies, waits for them, and re-layouts: 5.84 us -> 1.31 us
  Pallas kernels: 67 us -> 68.7 us
  waiting for transfers between devices: 4.09 us -> 3.07 us
    unnamed x18 -> x8, local copies, waits for them, and re-layouts: 5.84 us -> 1.31 us
    pallas_call x3, Pallas kernels: 9.08 us -> 10.6 us  [attend(): pl.pallas_call(functools.partial(attend_kernel, offsets), out_shape=(piec...]
    ppermute x3, waiting for transfers between devices: 4.09 us -> 3.07 us  [send(): return lax.ppermute(piece, ('blk', 'kv'), pairs_of(*offset))]
  transfers between devices with their start and end apart: 3 -> 3, of which waited for: 2 -> 2; matrix products, arithmetic and copies ran while one was open for 0% -> 0% of each run, Pallas kernels for 6% -> 8%
where the time goes in v5:
time: 76.2 us; the launch traced here: 76.6 us
  Pallas kernels  68.7 us (90%)
  starting transfers between devices  3.43 us (5%)
  waiting for transfers between devices  3.07 us (4%)
  local copies, waits for them, and re-layouts  1.31 us (2%)
    pallas_call x1, Pallas kernels, on_device(): pl.pallas_call(gather_kernel, out_shape=(jax.ShapeDtypeStruct((4 * rows,...  56 us
    pallas_call x3, Pallas kernels, attend(): pl.pallas_call(functools.partial(attend_kernel, offsets), out_shape=(piec...  10.6 us
    ppermute x3, starting transfers between devices, send(): return lax.ppermute(piece, ('blk', 'kv'), pairs_of(*offset))  3.43 us
    ppermute x3, waiting for transfers between devices, send(): return lax.ppermute(piece, ('blk', 'kv'), pairs_of(*offset))  3.07 us
    pallas_call x1, Pallas kernels, on_device(): pl.pallas_call(assemble_kernel, out_shape=jax.ShapeDtypeStruct((rows, KV_...  2.06 us
  transfers between devices with their start and end apart: 3, of which 2 were waited for; matrix products, arithmetic and copies ran while one was open for 0% of the time, Pallas kernels for 8%

profile of v5, /device:TPU:0, one launch (start us, length us, event | category | flops | bytes accessed | tf_op | source)
XLA Modules:
  0.0 76.6 jit_solution(1343325701241348201)
XLA Ops:
  0.0 56.0 %gather_heads.1 = (bf16[512,640]{1,0:T(8,128)(2,1)S(1)}, bf16[8192,128]{1,0:T(8,128)(2,1)S(1)}, bf16[8192,128]{1,0:T(8,128)(2,1)S(1)}, s32[16,64]{1,0:T(8,128)S(1)}, s32[16]{0:T(128)S(1)}) custom-call(bf16[128,2560]{1,0:T(8,128)(2,1)} %q_ref.1, bf16[512,512]{1,0:T(8,128)(2,1)} %k_ref.1, bf16[512,512]{1,0:T(8,128)(2,1)} %v_ref.1, s32[16,64]{1,0:T(8,128)} %ancestry.1, ...), custom_call_target="tpu_custom_call" | custom-call | tf_op jit(solution)/shard_map/gather_heads/pallas_call | solution.py:315
  56.1 4.6 %attend_far.1 = (bf16[128,640]{1,0:T(8,128)(2,1)S(1)}, bf16[128,640]{1,0:T(8,128)(2,1)S(1)}) custom-call(s32[16,64]{1,0:T(8,128)S(1)} %get-tuple-element.12.ancestry, s32[16]{0:T(128)S(1)} %get-tuple-element.13.leaf_tiles, bf16[512,640]{1,0:T(8,128)(2,1)S(1)} %get-tuple-element.14.q_ref, bf16[8192,128]{1,0:T(8,128)(2,1)S(1)} %get-tuple-element.15.k_ref, ...), custom_call_target="tpu_custom_call" | custom-call | flops 1342177280 | bytes 4194304 | tf_op jit(solution)/shard_map/attend_far/pallas_call | solution.py:341
  60.7 0.4 collective-permute-start
  61.1 2.9 %collective-permute-start.1 = (bf16[128,640]{1,0:T(8,128)(2,1)S(1)}, bf16[128,640]{1,0:T(8,128)(2,1)S(1)}, u32[]{:S(2)}, u32[]{:S(2)}) collective-permute-start(bf16[128,640]{1,0:T(8,128)(2,1)S(1)} %get-tuple-element.18), channel_id=1, source_target_pairs={{0,1},{1,0},{2,3},{3,2},{4,5},{5,4},{6,7},{7,6},{8,9},{9,8},{10,11... | collective-permute-start | bytes 491528 | tf_op jit(solution)/shard_map/ppermute | solution.py:361
  64.1 3.3 %attend_near.1 = bf16[128,640]{1,0:T(8,128)(2,1)S(1)} custom-call(s32[16,64]{1,0:T(8,128)S(1)} %get-tuple-element.12.ancestry, s32[16]{0:T(128)S(1)} %get-tuple-element.13.leaf_tiles, bf16[512,640]{1,0:T(8,128)(2,1)S(1)} %get-tuple-element.14.q_ref, bf16[8192,128]{1,0:T(8,128)(2,1)S(1)} %get-tuple-element.15.k_ref, bf16[8192,128]{1,0:T(8,128)(2,1)S(1)} %get-tuple-element.16.v_ref), custom_call_target="tpu_custom_call" | custom-call | flops 671088640 | bytes 4194304 | tf_op jit(solution)/shard_map/attend_near/pallas_call | solution.py:341
  67.3 0.1 collective-permute-start.2
  67.4 2.7 %attend_own.1.refs_0_ = bf16[128,640]{1,0:T(8,128)(2,1)S(1)} custom-call(s32[16,64]{1,0:T(8,128)S(1)} %get-tuple-element.12.ancestry, s32[16]{0:T(128)S(1)} %get-tuple-element.13.leaf_tiles, bf16[512,640]{1,0:T(8,128)(2,1)S(1)} %get-tuple-element.14.q_ref, bf16[8192,128]{1,0:T(8,128)(2,1)S(1)} %get-tuple-element.15.k_ref, ...), custom_call_target="tpu_custom_call" | custom-call | flops 671088640 | bytes 4194304 | tf_op jit(solution)/shard_map/attend_own/pallas_call | solution.py:341
  70.1 0.0 copy-start
  70.2 0.6 copy-done
  70.8 0.0 collective-permute-done.refs_1_
  70.8 0.0 copy-start.1
  70.8 1.8 %collective-permute-done.1.refs_2_ = bf16[128,640]{1,0:T(8,128)(2,1)S(1)} collective-permute-done((bf16[128,640]{1,0:T(8,128)(2,1)S(1)}, bf16[128,640]{1,0:T(8,128)(2,1)S(1)}, u32[]{:S(2)}, u32[]{:S(2)}) %collective-permute-start.1) | collective-permute-done | bytes 163872 | tf_op jit(solution)/shard_map/ppermute | solution.py:361
  72.6 0.0 copy-start.2
  72.6 1.3 %collective-permute-done.2.refs_3_ = bf16[128,640]{1,0:T(8,128)(2,1)S(1)} collective-permute-done((bf16[128,640]{1,0:T(8,128)(2,1)S(1)}, bf16[128,640]{1,0:T(8,128)(2,1)S(1)}, u32[]{:S(2)}, u32[]{:S(2)}) %collective-permute-start.2) | collective-permute-done | bytes 163872 | tf_op jit(solution)/shard_map/ppermute | solution.py:361
  73.9 0.0 copy-done.1
  73.9 0.0 copy-done.2
  73.9 0.0 copy-start.3
  73.9 0.7 copy-done.3
  74.5 2.1 %assemble_heads.1 = bf16[128,2560]{1,0:T(8,128)(2,1)} custom-call(bf16[128,640]{1,0:T(8,128)(2,1)} %copy-done, bf16[128,640]{1,0:T(8,128)(2,1)} %copy-done.1, bf16[128,640]{1,0:T(8,128)(2,1)} %copy-done.2, bf16[128,640]{1,0:T(8,128)(2,1)} %copy-done.3), custom_call_target="tpu_custom_call" | custom-call | tf_op jit(solution)/shard_map/assemble_heads/pallas_call | solution.py:369
Async XLA Ops:
  60.7 10.1 %collective-permute-start = (bf16[128,640]{1,0:T(8,128)(2,1)S(1)}, bf16[128,640]{1,0:T(8,128)(2,1)S(1)}, u32[]{:S(2)}, u32[]{:S(2)}) collective-permute-start(bf16[128,640]{1,0:T(8,128)(2,1)S(1)} %get-tuple-element.17), channel_id=1, source_target_pairs={{0,9},{1,8},{2,11},{3,10},{4,13},{5,12},{6,15},{7,14},{8,1},{9,0},... | collective-permute-start | bytes 491528 | tf_op jit(solution)/shard_map/ppermute | solution.py:361
  61.1 11.4 %collective-permute-start.1 = (bf16[128,640]{1,0:T(8,128)(2,1)S(1)}, bf16[128,640]{1,0:T(8,128)(2,1)S(1)}, u32[]{:S(2)}, u32[]{:S(2)}) collective-permute-start(bf16[128,640]{1,0:T(8,128)(2,1)S(1)} %get-tuple-element.18), channel_id=1, source_target_pairs={{0,1},{1,0},{2,3},{3,2},{4,5},{5,4},{6,7},{7,6},{8,9},{9,8},{10,11... | collective-permute-start | bytes 491528 | tf_op jit(solution)/shard_map/ppermute | solution.py:361
  67.3 6.5 %collective-permute-start.2 = (bf16[128,640]{1,0:T(8,128)(2,1)S(1)}, bf16[128,640]{1,0:T(8,128)(2,1)S(1)}, u32[]{:S(2)}, u32[]{:S(2)}) collective-permute-start(bf16[128,640]{1,0:T(8,128)(2,1)S(1)} %attend_near.1), channel_id=1, source_target_pairs={{0,8},{1,9},{2,10},{3,11},{4,12},{5,13},{6,14},{7,15},{8,0},{9,1},... | collective-permute-start | bytes 491528 | tf_op jit(solution)/shard_map/ppermute | solution.py:361
  70.1 0.7 copy-start
  70.8 3.1 %copy-start.1 = (bf16[128,640]{1,0:T(8,128)(2,1)}, bf16[128,640]{1,0:T(8,128)(2,1)S(1)}, u32[]{:S(2)}) copy-start(bf16[128,640]{1,0:T(8,128)(2,1)S(1)} %collective-permute-done.refs_1_) | copy-start | bytes 491524
  72.6 1.3 %copy-start.2 = (bf16[128,640]{1,0:T(8,128)(2,1)}, bf16[128,640]{1,0:T(8,128)(2,1)S(1)}, u32[]{:S(2)}) copy-start(bf16[128,640]{1,0:T(8,128)(2,1)S(1)} %collective-permute-done.1.refs_2_) | copy-start | bytes 491524
  73.9 0.7 copy-start.3

commit v6 on v5

--- a/solution.py
+++ b/solution.py
@@ -371,6 +371,7 @@
         out_shape=jax.ShapeDtypeStruct((rows, KV_HEADS * WIDE), bf16),
         in_specs=[vmem] * 4,
         out_specs=vmem,
+        compiler_params=pltpu.CompilerParams(vmem_limit_bytes=8 * 1024 * 1024),
         name="assemble_heads",
     )(own, *arrived)
 

time: 76.2 us -> 74.8 us (0.982)
  Pallas kernels: 68.7 us -> 66.6 us
  local copies, waits for them, and re-layouts: 1.31 us -> 0 us
  waiting for transfers between devices: 3.07 us -> 4.3 us
    unnamed x8 -> x0, local copies, waits for them, and re-layouts: 1.31 us -> none
    ppermute x3, waiting for transfers between devices: 3.07 us -> 4.3 us  [send(): return lax.ppermute(piece, ('blk', 'kv'), pairs_of(*offset))]
    pallas_call x1, Pallas kernels: 2.06 us -> 0.91 us  [on_device(): pl.pallas_call(assemble_kernel, out_shape=jax.ShapeDtypeStruct((rows, KV_...]
    pallas_call x3, Pallas kernels: 10.6 us -> 9.6 us  [attend(): pl.pallas_call(functools.partial(attend_kernel, offsets), out_shape=(piec...]
  transfers between devices with their start and end apart: 3 -> 3, of which waited for: 2 -> 2; matrix products, arithmetic and copies ran while one was open for 0% -> 0% of each run, Pallas kernels for 8% -> 6%
where the time goes in v6:
time: 74.8 us; the launch traced here: 74.5 us
  Pallas kernels  66.6 us (89%)
  waiting for transfers between devices  4.3 us (6%)
  starting transfers between devices  3.59 us (5%)
    pallas_call x1, Pallas kernels, on_device(): pl.pallas_call(gather_kernel, out_shape=(jax.ShapeDtypeStruct((4 * rows,...  56 us
    pallas_call x3, Pallas kernels, attend(): pl.pallas_call(functools.partial(attend_kernel, offsets), out_shape=(piec...  9.6 us
    ppermute x3, waiting for transfers between devices, send(): return lax.ppermute(piece, ('blk', 'kv'), pairs_of(*offset))  4.3 us
    ppermute x3, starting transfers between devices, send(): return lax.ppermute(piece, ('blk', 'kv'), pairs_of(*offset))  3.59 us
  transfers between devices with their start and end apart: 3, of which 2 were waited for; matrix products, arithmetic and copies ran while one was open for 0% of the time, Pallas kernels for 6%

profile of v6, /device:TPU:0, one launch (start us, length us, event | category | flops | bytes accessed | tf_op | source)
XLA Modules:
  0.0 74.5 jit_solution(8748307299396599443)
XLA Ops:
  0.0 56.0 %gather_heads.1 = (bf16[512,640]{1,0:T(8,128)(2,1)S(1)}, bf16[8192,128]{1,0:T(8,128)(2,1)S(1)}, bf16[8192,128]{1,0:T(8,128)(2,1)S(1)}, s32[16,64]{1,0:T(8,128)S(1)}, s32[16]{0:T(128)S(1)}) custom-call(bf16[128,2560]{1,0:T(8,128)(2,1)} %q_ref.1, bf16[512,512]{1,0:T(8,128)(2,1)} %k_ref.1, bf16[512,512]{1,0:T(8,128)(2,1)} %v_ref.1, s32[16,64]{1,0:T(8,128)} %ancestry.1, ...), custom_call_target="tpu_custom_call" | custom-call | tf_op jit(solution)/shard_map/gather_heads/pallas_call | solution.py:315
  56.1 5.1 %attend_far.1 = (bf16[128,640]{1,0:T(8,128)(2,1)S(1)}, bf16[128,640]{1,0:T(8,128)(2,1)S(1)}) custom-call(s32[16,64]{1,0:T(8,128)S(1)} %get-tuple-element.12.ancestry, s32[16]{0:T(128)S(1)} %get-tuple-element.13.leaf_tiles, bf16[512,640]{1,0:T(8,128)(2,1)S(1)} %get-tuple-element.14.q_ref, bf16[8192,128]{1,0:T(8,128)(2,1)S(1)} %get-tuple-element.15.k_ref, ...), custom_call_target="tpu_custom_call" | custom-call | flops 1342177280 | bytes 4194304 | tf_op jit(solution)/shard_map/attend_far/pallas_call | solution.py:341
  61.2 0.1 collective-permute-start
  61.3 3.3 %collective-permute-start.1 = (bf16[128,640]{1,0:T(8,128)(2,1)S(1)}, bf16[128,640]{1,0:T(8,128)(2,1)S(1)}, u32[]{:S(2)}, u32[]{:S(2)}) collective-permute-start(bf16[128,640]{1,0:T(8,128)(2,1)S(1)} %get-tuple-element.18), channel_id=1, source_target_pairs={{0,1},{1,0},{2,3},{3,2},{4,5},{5,4},{6,7},{7,6},{8,9},{9,8},{10,11... | collective-permute-start | bytes 491528 | tf_op jit(solution)/shard_map/ppermute | solution.py:361
  64.6 2.2 %attend_near.1 = bf16[128,640]{1,0:T(8,128)(2,1)S(1)} custom-call(s32[16,64]{1,0:T(8,128)S(1)} %get-tuple-element.12.ancestry, s32[16]{0:T(128)S(1)} %get-tuple-element.13.leaf_tiles, bf16[512,640]{1,0:T(8,128)(2,1)S(1)} %get-tuple-element.14.q_ref, bf16[8192,128]{1,0:T(8,128)(2,1)S(1)} %get-tuple-element.15.k_ref, bf16[8192,128]{1,0:T(8,128)(2,1)S(1)} %get-tuple-element.16.v_ref), custom_call_target="tpu_custom_call" | custom-call | flops 671088640 | bytes 4194304 | tf_op jit(solution)/shard_map/attend_near/pallas_call | solution.py:341
  66.8 0.3 collective-permute-start.2
  67.1 2.2 %attend_own.1.refs_0_ = bf16[128,640]{1,0:T(8,128)(2,1)S(1)} custom-call(s32[16,64]{1,0:T(8,128)S(1)} %get-tuple-element.12.ancestry, s32[16]{0:T(128)S(1)} %get-tuple-element.13.leaf_tiles, bf16[512,640]{1,0:T(8,128)(2,1)S(1)} %get-tuple-element.14.q_ref, bf16[8192,128]{1,0:T(8,128)(2,1)S(1)} %get-tuple-element.15.k_ref, ...), custom_call_target="tpu_custom_call" | custom-call | flops 671088640 | bytes 4194304 | tf_op jit(solution)/shard_map/attend_own/pallas_call | solution.py:341
  69.3 0.0 collective-permute-done.refs_1_
  69.3 3.4 %collective-permute-done.1.refs_2_ = bf16[128,640]{1,0:T(8,128)(2,1)S(1)} collective-permute-done((bf16[128,640]{1,0:T(8,128)(2,1)S(1)}, bf16[128,640]{1,0:T(8,128)(2,1)S(1)}, u32[]{:S(2)}, u32[]{:S(2)}) %collective-permute-start.1) | collective-permute-done | bytes 163872 | tf_op jit(solution)/shard_map/ppermute | solution.py:361
  72.7 0.9 %collective-permute-done.2.refs_3_ = bf16[128,640]{1,0:T(8,128)(2,1)S(1)} collective-permute-done((bf16[128,640]{1,0:T(8,128)(2,1)S(1)}, bf16[128,640]{1,0:T(8,128)(2,1)S(1)}, u32[]{:S(2)}, u32[]{:S(2)}) %collective-permute-start.2) | collective-permute-done | bytes 163872 | tf_op jit(solution)/shard_map/ppermute | solution.py:361
  73.6 0.9 %assemble_heads.1 = bf16[128,2560]{1,0:T(8,128)(2,1)} custom-call(bf16[128,640]{1,0:T(8,128)(2,1)S(1)} %attend_own.1.refs_0_, bf16[128,640]{1,0:T(8,128)(2,1)S(1)} %collective-permute-done.refs_1_, bf16[128,640]{1,0:T(8,128)(2,1)S(1)} %collective-permute-done.1.refs_2_, bf16[128,640]{1,0:T(8,128)(2,1)S(1)} %collective-permute-done.2.refs_3_), custom_call_target="tpu_custom_call" | custom-call | tf_op jit(solution)/shard_map/assemble_heads/pallas_call | solution.py:369
Async XLA Ops:
  61.2 8.1 %collective-permute-start = (bf16[128,640]{1,0:T(8,128)(2,1)S(1)}, bf16[128,640]{1,0:T(8,128)(2,1)S(1)}, u32[]{:S(2)}, u32[]{:S(2)}) collective-permute-start(bf16[128,640]{1,0:T(8,128)(2,1)S(1)} %get-tuple-element.17), channel_id=1, source_target_pairs={{0,9},{1,8},{2,11},{3,10},{4,13},{5,12},{6,15},{7,14},{8,1},{9,0},... | collective-permute-start | bytes 491528 | tf_op jit(solution)/shard_map/ppermute | solution.py:361
  61.3 11.4 %collective-permute-start.1 = (bf16[128,640]{1,0:T(8,128)(2,1)S(1)}, bf16[128,640]{1,0:T(8,128)(2,1)S(1)}, u32[]{:S(2)}, u32[]{:S(2)}) collective-permute-start(bf16[128,640]{1,0:T(8,128)(2,1)S(1)} %get-tuple-element.18), channel_id=1, source_target_pairs={{0,1},{1,0},{2,3},{3,2},{4,5},{5,4},{6,7},{7,6},{8,9},{9,8},{10,11... | collective-permute-start | bytes 491528 | tf_op jit(solution)/shard_map/ppermute | solution.py:361
  66.8 6.8 %collective-permute-start.2 = (bf16[128,640]{1,0:T(8,128)(2,1)S(1)}, bf16[128,640]{1,0:T(8,128)(2,1)S(1)}, u32[]{:S(2)}, u32[]{:S(2)}) collective-permute-start(bf16[128,640]{1,0:T(8,128)(2,1)S(1)} %attend_near.1), channel_id=1, source_target_pairs={{0,8},{1,9},{2,10},{3,11},{4,12},{5,13},{6,14},{7,15},{8,0},{9,1},... | collective-permute-start | bytes 491528 | tf_op jit(solution)/shard_map/ppermute | solution.py:361

commit v7 on v6

--- a/solution.py
+++ b/solution.py
@@ -224,27 +224,30 @@
 
     for j in tiles:
         rows = aligned(head_of(*spots[j]), TILE)
-        query = jnp.concatenate(
-            [q_ref[rows, pl.ds(g * DH, DH)] for g in range(GROUP)], axis=0
-        )
+        queries = [q_ref[rows, pl.ds(g * DH, DH)] for g in range(GROUP)]
+        parts = [pl.ds(g * TILE, TILE) for g in range(GROUP)]
         count = counts[j]
         steps = (count + 1) // 2
 
         def score(i, first):
-            raw = lax.dot_general(
-                query, pair_of(k_ref, j, i), (((1,), (1,)), ((), ())),
-                preferred_element_type=jnp.float32,
-            )
-            left = raw[:, :TILE]
-            if first:
-                q_in = lax.broadcasted_iota(jnp.int32, (WIDE, TILE), 0) % TILE
-                s_in = lax.broadcasted_iota(jnp.int32, (WIDE, TILE), 1)
-                left = jnp.where(s_in <= q_in, left, NEG)
-            right = raw[:, TILE:] + jnp.where(2 * i + 1 < count, 0.0, NEG)
-            scores[i, :, :TILE] = left
-            scores[i, :, TILE:] = right
-            best = jnp.maximum(left, right)
-            peak_ref[...] = best if first else jnp.maximum(peak_ref[...], best)
+            pair = pair_of(k_ref, j, i)
+            for g in range(GROUP):
+                raw = lax.dot_general(
+                    queries[g], pair, (((1,), (1,)), ((), ())),
+                    preferred_element_type=jnp.float32,
+                )
+                left = raw[:, :TILE]
+                if first:
+                    q_in = lax.broadcasted_iota(jnp.int32, (TILE, TILE), 0)
+                    s_in = lax.broadcasted_iota(jnp.int32, (TILE, TILE), 1)
+                    left = jnp.where(s_in <= q_in, left, NEG)
+                right = raw[:, TILE:] + jnp.where(2 * i + 1 < count, 0.0, NEG)
+                scores[i, parts[g], :TILE] = left
+                scores[i, parts[g], TILE:] = right
+                best = jnp.maximum(left, right)
+                peak_ref[parts[g], :] = (
+                    best if first else jnp.maximum(peak_ref[parts[g], :], best)
+                )
 
         score(0, True)
 
@@ -257,16 +260,19 @@
         )
 
         def weigh(i, first):
-            peak = peak_ref[...]
-            left = jnp.exp2((scores[i, :, :TILE] - peak) * EXP2_SCALE)
-            right = jnp.exp2((scores[i, :, TILE:] - peak) * EXP2_SCALE)
-            rounded = jnp.concatenate(
-                [left.astype(jnp.bfloat16), right.astype(jnp.bfloat16)], axis=1
-            )
-            update = jnp.dot(rounded, pair_of(v_ref, j, i), preferred_element_type=jnp.float32)
-            both = left + right
-            total_ref[...] = both if first else total_ref[...] + both
-            sum_ref[...] = update if first else sum_ref[...] + update
+            pair = pair_of(v_ref, j, i)
+            for g in range(GROUP):
+                part = parts[g]
+                peak = peak_ref[part, :]
+                left = jnp.exp2((scores[i, part, :TILE] - peak) * EXP2_SCALE)
+                right = jnp.exp2((scores[i, part, TILE:] - peak) * EXP2_SCALE)
+                rounded = jnp.concatenate(
+                    [left.astype(jnp.bfloat16), right.astype(jnp.bfloat16)], axis=1
+                )
+                update = jnp.dot(rounded, pair, preferred_element_type=jnp.float32)
+                both = left + right
+                total_ref[part, :] = both if first else total_ref[part, :] + both
+                sum_ref[part, :] = update if first else sum_ref[part, :] + update
 
         weigh(0, True)
 

time: 74.8 us -> 75.2 us (level)
  transfers between devices with their start and end apart: 3 -> 3, of which waited for: 2 -> 2; matrix products, arithmetic and copies ran while one was open for 0% -> 0% of each run, Pallas kernels for 6% -> 7%
where the time goes in v7:
time: 75.2 us; the launch traced here: 75.3 us
  Pallas kernels  67.1 us (89%)
  waiting for transfers between devices  4.74 us (6%)
  starting transfers between devices  3.4 us (5%)
    pallas_call x1, Pallas kernels, on_device(): pl.pallas_call(gather_kernel, out_shape=(jax.ShapeDtypeStruct((4 * rows,...  56 us
    pallas_call x3, Pallas kernels, attend(): pl.pallas_call(functools.partial(attend_kernel, offsets), out_shape=(piec...  10.1 us
    ppermute x3, waiting for transfers between devices, send(): return lax.ppermute(piece, ('blk', 'kv'), pairs_of(*offset))  4.74 us
    ppermute x3, starting transfers between devices, send(): return lax.ppermute(piece, ('blk', 'kv'), pairs_of(*offset))  3.4 us
  transfers between devices with their start and end apart: 3, of which 2 were waited for; matrix products, arithmetic and copies ran while one was open for 0% of the time, Pallas kernels for 7%

profile of v7, /device:TPU:0, one launch (start us, length us, event | category | flops | bytes accessed | tf_op | source)
XLA Modules:
  0.0 75.3 jit_solution(8938961057550621518)
XLA Ops:
  0.0 56.0 %gather_heads.1 = (bf16[512,640]{1,0:T(8,128)(2,1)S(1)}, bf16[8192,128]{1,0:T(8,128)(2,1)S(1)}, bf16[8192,128]{1,0:T(8,128)(2,1)S(1)}, s32[16,64]{1,0:T(8,128)S(1)}, s32[16]{0:T(128)S(1)}) custom-call(bf16[128,2560]{1,0:T(8,128)(2,1)} %q_ref.1, bf16[512,512]{1,0:T(8,128)(2,1)} %k_ref.1, bf16[512,512]{1,0:T(8,128)(2,1)} %v_ref.1, s32[16,64]{1,0:T(8,128)} %ancestry.1, ...), custom_call_target="tpu_custom_call" | custom-call | tf_op jit(solution)/shard_map/gather_heads/pallas_call | solution.py:321
  56.1 5.2 %attend_far.1 = (bf16[128,640]{1,0:T(8,128)(2,1)S(1)}, bf16[128,640]{1,0:T(8,128)(2,1)S(1)}) custom-call(s32[16,64]{1,0:T(8,128)S(1)} %get-tuple-element.12.ancestry, s32[16]{0:T(128)S(1)} %get-tuple-element.13.leaf_tiles, bf16[512,640]{1,0:T(8,128)(2,1)S(1)} %get-tuple-element.14.q_ref, bf16[8192,128]{1,0:T(8,128)(2,1)S(1)} %get-tuple-element.15.k_ref, ...), custom_call_target="tpu_custom_call" | custom-call | flops 1342177280 | bytes 4194304 | tf_op jit(solution)/shard_map/attend_far/pallas_call | solution.py:347
  61.2 0.1 collective-permute-start
  61.3 3.3 %collective-permute-start.1 = (bf16[128,640]{1,0:T(8,128)(2,1)S(1)}, bf16[128,640]{1,0:T(8,128)(2,1)S(1)}, u32[]{:S(2)}, u32[]{:S(2)}) collective-permute-start(bf16[128,640]{1,0:T(8,128)(2,1)S(1)} %get-tuple-element.18), channel_id=1, source_target_pairs={{0,1},{1,0},{2,3},{3,2},{4,5},{5,4},{6,7},{7,6},{8,9},{9,8},{10,11... | collective-permute-start | bytes 491528 | tf_op jit(solution)/shard_map/ppermute | solution.py:367
  64.6 3.2 %attend_near.1 = bf16[128,640]{1,0:T(8,128)(2,1)S(1)} custom-call(s32[16,64]{1,0:T(8,128)S(1)} %get-tuple-element.12.ancestry, s32[16]{0:T(128)S(1)} %get-tuple-element.13.leaf_tiles, bf16[512,640]{1,0:T(8,128)(2,1)S(1)} %get-tuple-element.14.q_ref, bf16[8192,128]{1,0:T(8,128)(2,1)S(1)} %get-tuple-element.15.k_ref, bf16[8192,128]{1,0:T(8,128)(2,1)S(1)} %get-tuple-element.16.v_ref), custom_call_target="tpu_custom_call" | custom-call | flops 671088640 | bytes 4194304 | tf_op jit(solution)/shard_map/attend_near/pallas_call | solution.py:347
  67.8 0.1 collective-permute-start.2
  67.9 1.7 %attend_own.1.refs_0_ = bf16[128,640]{1,0:T(8,128)(2,1)S(1)} custom-call(s32[16,64]{1,0:T(8,128)S(1)} %get-tuple-element.12.ancestry, s32[16]{0:T(128)S(1)} %get-tuple-element.13.leaf_tiles, bf16[512,640]{1,0:T(8,128)(2,1)S(1)} %get-tuple-element.14.q_ref, bf16[8192,128]{1,0:T(8,128)(2,1)S(1)} %get-tuple-element.15.k_ref, ...), custom_call_target="tpu_custom_call" | custom-call | flops 671088640 | bytes 4194304 | tf_op jit(solution)/shard_map/attend_own/pallas_call | solution.py:347
  69.6 0.0 collective-permute-done.refs_1_
  69.6 3.5 %collective-permute-done.1.refs_2_ = bf16[128,640]{1,0:T(8,128)(2,1)S(1)} collective-permute-done((bf16[128,640]{1,0:T(8,128)(2,1)S(1)}, bf16[128,640]{1,0:T(8,128)(2,1)S(1)}, u32[]{:S(2)}, u32[]{:S(2)}) %collective-permute-start.1) | collective-permute-done | bytes 163872 | tf_op jit(solution)/shard_map/ppermute | solution.py:367
  73.1 1.3 %collective-permute-done.2.refs_3_ = bf16[128,640]{1,0:T(8,128)(2,1)S(1)} collective-permute-done((bf16[128,640]{1,0:T(8,128)(2,1)S(1)}, bf16[128,640]{1,0:T(8,128)(2,1)S(1)}, u32[]{:S(2)}, u32[]{:S(2)}) %collective-permute-start.2) | collective-permute-done | bytes 163872 | tf_op jit(solution)/shard_map/ppermute | solution.py:367
  74.4 0.9 %assemble_heads.1 = bf16[128,2560]{1,0:T(8,128)(2,1)} custom-call(bf16[128,640]{1,0:T(8,128)(2,1)S(1)} %attend_own.1.refs_0_, bf16[128,640]{1,0:T(8,128)(2,1)S(1)} %collective-permute-done.refs_1_, bf16[128,640]{1,0:T(8,128)(2,1)S(1)} %collective-permute-done.1.refs_2_, bf16[128,640]{1,0:T(8,128)(2,1)S(1)} %collective-permute-done.2.refs_3_), custom_call_target="tpu_custom_call" | custom-call | tf_op jit(solution)/shard_map/assemble_heads/pallas_call | solution.py:375
Async XLA Ops:
  61.2 8.4 %collective-permute-start = (bf16[128,640]{1,0:T(8,128)(2,1)S(1)}, bf16[128,640]{1,0:T(8,128)(2,1)S(1)}, u32[]{:S(2)}, u32[]{:S(2)}) collective-permute-start(bf16[128,640]{1,0:T(8,128)(2,1)S(1)} %get-tuple-element.17), channel_id=1, source_target_pairs={{0,9},{1,8},{2,11},{3,10},{4,13},{5,12},{6,15},{7,14},{8,1},{9,0},... | collective-permute-start | bytes 491528 | tf_op jit(solution)/shard_map/ppermute | solution.py:367
  61.3 11.8 %collective-permute-start.1 = (bf16[128,640]{1,0:T(8,128)(2,1)S(1)}, bf16[128,640]{1,0:T(8,128)(2,1)S(1)}, u32[]{:S(2)}, u32[]{:S(2)}) collective-permute-start(bf16[128,640]{1,0:T(8,128)(2,1)S(1)} %get-tuple-element.18), channel_id=1, source_target_pairs={{0,1},{1,0},{2,3},{3,2},{4,5},{5,4},{6,7},{7,6},{8,9},{9,8},{10,11... | collective-permute-start | bytes 491528 | tf_op jit(solution)/shard_map/ppermute | solution.py:367
  67.8 6.6 %collective-permute-start.2 = (bf16[128,640]{1,0:T(8,128)(2,1)S(1)}, bf16[128,640]{1,0:T(8,128)(2,1)S(1)}, u32[]{:S(2)}, u32[]{:S(2)}) collective-permute-start(bf16[128,640]{1,0:T(8,128)(2,1)S(1)} %attend_near.1), channel_id=1, source_target_pairs={{0,8},{1,9},{2,10},{3,11},{4,12},{5,13},{6,14},{7,15},{8,0},{9,1},... | collective-permute-start | bytes 491528 | tf_op jit(solution)/shard_map/ppermute | solution.py:367
